TPU v7x, 32 devices: a whole 2x2x4 slice. The times are simulated.
32 devices in a mesh: pb: 4 (over y, x), pa: 8 (over z, core).
Axes of the slice: x: 2, y: 2, z: 4, core: 2. Of those that a mesh axis runs over, the one named last changes fastest.
Arguments:
- decoder_in: float32 [16, 20, 768], P('pb'), may hold values from -6 to 6
- encodings: bfloat16 [16, 4096, 768], P('pb', 'pa'), may hold values from -6 to 6
- out_grad: float32 [16, 20, 768], P('pb'), may hold values from -6 to 6
- passage_len: int32 [16], P('pb'), may hold values from 250 to 500, as said below
- passage_count: int32 [16], P('pb'), may hold values from 4 to 16, as said below
- buckets: int32 [20, 20], replicated, may hold values from 0 to 31
- self_query: bfloat16 [768, 768], P('pa'), may hold values from -0.21875 to 0.21875
- self_key: bfloat16 [768, 768], P('pa'), may hold values from -0.21875 to 0.21875
- self_value: bfloat16 [768, 768], P('pa'), may hold values from -0.21875 to 0.21875
- self_out: bfloat16 [768, 768], P('pa'), may hold values from -0.4375 to 0.4375
- cross_query: bfloat16 [768, 768], P('pa'), may hold values from -0.4375 to 0.4375
- cross_key: bfloat16 [768, 768], P('pa'), may hold values from -0.21875 to 0.21875
- cross_value: bfloat16 [768, 768], P('pa'), may hold values from -0.21875 to 0.21875
- cross_out: bfloat16 [768, 768], P('pa'), may hold values from -3.5 to 3.5
- ffn_expand: bfloat16 [768, 3072], P('pa'), may hold values from -0.21875 to 0.21875
- ffn_reduce: bfloat16 [3072, 768], P('pa'), may hold values from -0.15625 to 0.15625
- norm_self: float32 [768], replicated, may hold values from 0.5 to 1.5
- norm_cross: float32 [768], replicated, may hold values from 0.5 to 1.5
- norm_ffn: float32 [768], replicated, may hold values from 0.5 to 1.5
- bias_table: float32 [32, 12], replicated, may hold values from -4 to 4
Outputs:
- decoder_out: float32 [16, 20, 768], P('pb')
- decoder_grad: float32 [16, 20, 768], P('pb')
- encoding_grad: float32 [16, 4096, 768], P('pb', 'pa')
- grad_self_query: float32 [768, 768], P('pa')
- grad_self_key: float32 [768, 768], P('pa')
- grad_self_value: float32 [768, 768], P('pa')
- grad_self_out: float32 [768, 768], P('pa')
- grad_cross_query: float32 [768, 768], P('pa')
- grad_cross_key: float32 [768, 768], P('pa')
- grad_cross_value: float32 [768, 768], P('pa')
- grad_cross_out: float32 [768, 768], P('pa')
- grad_ffn_expand: float32 [768, 3072], P('pa')
- grad_ffn_reduce: float32 [3072, 768], P('pa')
- grad_norm_self: float32 [768], replicated
- grad_norm_cross: float32 [768], replicated
- grad_norm_ffn: float32 [768], replicated
- grad_bias_table: float32 [32, 12], replicated
Inputs may be any that keep to these rules, and one draw needn't show every extreme that they name: `passage_len`: each question's passages all have one length, 250 or 500; in the first aligned block of 4 questions some question has short passages and fills every place, in the second some question has long ones and fills every place. `passage_count`: a question with passages of length L has between half and all of (4096 // 512) * (512 // L) passages; in every aligned block of 4 questions one question has all of them.
All inputs are finite; a program needn't handle non-finite values.
Results may differ from a plain program's by a relative error of at most 0.03.
Values may be sent and summed in bfloat16 or wider, within the bound.
A program may use at most 128 MiB of HBM per device.

v0:
```python
import jax
import jax.numpy as jnp
from jax import lax
from jax.sharding import PartitionSpec as P

epsilon = 1e-06
highest = lax.Precision.HIGHEST
masked_score = -1e30


def product(left, right):
    return jnp.dot(left, right, preferred_element_type=jnp.float32)


def lowered(value):
    return value.astype(jnp.bfloat16)


def norm_forward(value):
    factor = lax.rsqrt(jnp.mean(value * value, -1, keepdims=True) + epsilon)
    return (value * factor, factor)


def norm_backward(grad_out, normal, factor, gain):
    inner_term = grad_out * gain
    grad_in = factor * (inner_term - normal * jnp.mean(inner_term * normal, -1, keepdims=True))
    grad_gain = jnp.sum(grad_out * normal, (0, 1))
    return (grad_in, grad_gain)


def activate(value):
    return jax.nn.gelu(value, approximate=True)


def shard_grad(inputs, grad_rows, device_place, row_count):
    sliced = lax.dynamic_slice_in_dim(inputs, device_place * row_count, row_count, 2)
    return jnp.einsum("qak,qae->ke", sliced, grad_rows, preferred_element_type=jnp.float32)


def shards(
    decoder_in,
    encodings,
    out_grad,
    passage_len,
    passage_count,
    buckets,
    self_query,
    self_key,
    self_value,
    self_out,
    cross_query,
    cross_key,
    cross_value,
    cross_out,
    ffn_expand,
    ffn_reduce,
    norm_self,
    norm_cross,
    norm_ffn,
    bias_table,
):
    wide_count = lax.axis_size("pa")
    device_place = lax.axis_index("pa")
    stacked = jnp.stack(
        [self_query, self_key, self_value, self_out, cross_query, cross_key, cross_value, cross_out]
    )
    squares, expand_full, reduce_full = (
        lax.all_gather(stacked, "pa", axis=1, tiled=True),
        lax.all_gather(ffn_expand, "pa", axis=0, tiled=True),
        lax.all_gather(ffn_reduce, "pa", axis=0, tiled=True),
    )
    query_self = squares[0]
    key_self = squares[1]
    value_self = squares[2]
    out_self = squares[3]
    query_cross = squares[4]
    key_cross = squares[5]
    value_cross = squares[6]
    out_cross = squares[7]
    questions, answer, model_width = decoder_in.shape
    head_count = bias_table.shape[1]
    head_size = model_width // head_count
    factor = head_size ** (-0.5)
    slot_rows = encodings.shape[1]
    rows_model = model_width // wide_count
    rows_hidden = expand_full.shape[1] // wide_count

    def heads_of(value):
        return value.reshape(value.shape[0], value.shape[1], head_count, head_size)

    normal_one, factor_one = norm_forward(decoder_in)
    hidden_one = lowered(normal_one * norm_self)
    query_heads = heads_of(lowered(product(hidden_one, query_self)))
    key_heads = heads_of(lowered(product(hidden_one, key_self)))
    value_heads = heads_of(lowered(product(hidden_one, value_self)))
    onehot = (buckets[:, :, None] == jnp.arange(bias_table.shape[0])[None, None, :]).astype(
        jnp.float32
    )
    bias_scores = jnp.einsum("ijb,bh->hij", onehot, bias_table, precision=highest)
    causal = jnp.arange(answer)[:, None] >= jnp.arange(answer)[None, :]
    scores = (
        jnp.einsum("qihd,qjhd->qhij", query_heads, key_heads, preferred_element_type=jnp.float32)
        * factor
        + bias_scores[None]
    )
    scores = jnp.where(causal[None, None], scores, masked_score)
    probabilities = jax.nn.softmax(scores, -1)
    weights_self = lowered(probabilities)
    mixed_self = lowered(
        jnp.einsum("qhij,qjhd->qihd", weights_self, value_heads, preferred_element_type=jnp.float32)
    ).reshape(questions, answer, model_width)
    resid_one = decoder_in + product(mixed_self, out_self)
    normal_two, factor_two = norm_forward(resid_one)
    hidden_two = lowered(normal_two * norm_cross)
    cquery = heads_of(lowered(product(hidden_two, query_cross)))
    per_device = slot_rows // passage_len
    held_count = jnp.clip(passage_count - device_place * per_device, 0, per_device)
    valid_rows = jnp.arange(slot_rows)[None, :] < (held_count * passage_len)[:, None]

    def project(encoded):
        ckeys = lowered(product(encoded, key_cross)).reshape(
            questions, slot_rows, head_count, head_size
        )
        cvalues = lowered(product(encoded, value_cross)).reshape(
            questions, slot_rows, head_count, head_size
        )
        cscores = (
            jnp.einsum("qihd,qjhd->qhij", cquery, ckeys, preferred_element_type=jnp.float32)
            * factor
        )
        cscores = jnp.where(valid_rows[:, None, None, :], cscores, masked_score)
        return (ckeys, cvalues, cscores)

    ckeys, cvalues, cscores = project(encodings)
    row_max = lax.pmax(jnp.max(cscores, -1), "pa")
    exp_weights = jnp.exp(cscores - row_max[..., None])
    part_num = jnp.einsum(
        "qhij,qjhd->qihd", lowered(exp_weights), cvalues, preferred_element_type=jnp.float32
    )
    part_total = jnp.sum(exp_weights, -1)
    numerator, totals = lax.psum((part_num, part_total), "pa")
    totals_t = jnp.transpose(totals, (0, 2, 1))[..., None]
    mixed_cross = lowered(numerator / totals_t).reshape(questions, answer, model_width)
    resid_two = resid_one + product(mixed_cross, out_cross)
    normal_three, factor_three = norm_forward(resid_two)
    hidden_three = lowered(normal_three * norm_ffn)
    pre_act = product(hidden_three, expand_full)
    activation = lowered(activate(pre_act))
    decoder_out = resid_two + product(activation, reduce_full)
    grad_z = lowered(out_grad)
    grad_reduce = shard_grad(activation, grad_z, device_place, rows_hidden)
    grad_act = jnp.einsum("qae,fe->qaf", grad_z, reduce_full, preferred_element_type=jnp.float32)
    unused_out, gelu_back = jax.vjp(activate, pre_act)
    grad_pre = lowered(gelu_back(grad_act)[0])
    grad_expand = shard_grad(hidden_three, grad_pre, device_place, rows_model)
    grad_three = jnp.einsum(
        "qaf,kf->qak", grad_pre, expand_full, preferred_element_type=jnp.float32
    )
    back_term, grad_gain_ffn = norm_backward(grad_three, normal_three, factor_three, norm_ffn)
    grad_two = out_grad + back_term
    grad_c = lowered(grad_two)
    grad_out_cross = shard_grad(mixed_cross, grad_c, device_place, rows_model)
    grad_mix = heads_of(
        lowered(jnp.einsum("qae,ke->qak", grad_c, out_cross, preferred_element_type=jnp.float32))
    )
    grad_mix_wide = grad_mix.astype(jnp.float32)
    grad_num = lowered(grad_mix_wide / totals_t)
    grad_tot = -jnp.sum(grad_mix_wide * numerator, -1) / (totals_t[..., 0] * totals_t[..., 0])
    ckeys, cvalues, cscores = project(encodings)
    exp_weights = jnp.exp(cscores - row_max[..., None])
    grad_expo = jnp.einsum("qihd,qjhd->qhij", grad_num, cvalues, preferred_element_type=jnp.float32)
    grad_expo = grad_expo + jnp.transpose(grad_tot, (0, 2, 1))[..., None]
    grad_score = lowered(exp_weights * grad_expo)
    part_query = (
        jnp.einsum("qhij,qjhd->qihd", grad_score, ckeys, preferred_element_type=jnp.float32)
        * factor
    )
    grad_cquery = lowered(lax.psum(part_query, "pa")).reshape(questions, answer, model_width)
    grad_ckeys = lowered(
        jnp.einsum("qhij,qihd->qjhd", grad_score, cquery, preferred_element_type=jnp.float32)
        * factor
    ).reshape(questions, slot_rows, model_width)
    grad_cvalues = lowered(
        jnp.einsum(
            "qhij,qihd->qjhd", lowered(exp_weights), grad_num, preferred_element_type=jnp.float32
        )
    ).reshape(questions, slot_rows, model_width)
    encoding_grad = jnp.einsum(
        "qse,ke->qsk", grad_ckeys, key_cross, preferred_element_type=jnp.float32
    )
    encoding_grad = encoding_grad + jnp.einsum(
        "qse,ke->qsk", grad_cvalues, value_cross, preferred_element_type=jnp.float32
    )
    full_key = jnp.einsum("qsk,qse->ke", encodings, grad_ckeys, preferred_element_type=jnp.float32)
    full_value = jnp.einsum(
        "qsk,qse->ke", encodings, grad_cvalues, preferred_element_type=jnp.float32
    )
    grad_query_cross = shard_grad(hidden_two, grad_cquery, device_place, rows_model)
    grad_hidden_two = jnp.einsum(
        "qae,ke->qak", grad_cquery, query_cross, preferred_element_type=jnp.float32
    )
    back_term, grad_gain_cross = norm_backward(grad_hidden_two, normal_two, factor_two, norm_cross)
    grad_one = grad_two + back_term
    grad_a = lowered(grad_one)
    grad_out_self = shard_grad(mixed_self, grad_a, device_place, rows_model)
    grad_smix = heads_of(
        lowered(jnp.einsum("qae,ke->qak", grad_a, out_self, preferred_element_type=jnp.float32))
    )
    grad_w = jnp.einsum(
        "qihd,qjhd->qhij", grad_smix, value_heads, preferred_element_type=jnp.float32
    )
    grad_s = lowered(probabilities * (grad_w - jnp.sum(grad_w * probabilities, -1, keepdims=True)))
    grad_table = jnp.einsum(
        "ijb,hij->bh", onehot, jnp.sum(grad_s.astype(jnp.float32), 0), precision=highest
    )
    grad_sq = lowered(
        jnp.einsum("qhij,qjhd->qihd", grad_s, key_heads, preferred_element_type=jnp.float32)
        * factor
    ).reshape(questions, answer, model_width)
    grad_sk = lowered(
        jnp.einsum("qhij,qihd->qjhd", grad_s, query_heads, preferred_element_type=jnp.float32)
        * factor
    ).reshape(questions, answer, model_width)
    grad_sv = lowered(
        jnp.einsum("qhij,qihd->qjhd", weights_self, grad_smix, preferred_element_type=jnp.float32)
    ).reshape(questions, answer, model_width)
    grad_query_self = shard_grad(hidden_one, grad_sq, device_place, rows_model)
    grad_key_self = shard_grad(hidden_one, grad_sk, device_place, rows_model)
    grad_value_self = shard_grad(hidden_one, grad_sv, device_place, rows_model)
    grad_hidden_one = jnp.einsum(
        "qae,ke->qak", grad_sq, query_self, preferred_element_type=jnp.float32
    )
    grad_hidden_one = grad_hidden_one + jnp.einsum(
        "qae,ke->qak", grad_sk, key_self, preferred_element_type=jnp.float32
    )
    grad_hidden_one = grad_hidden_one + jnp.einsum(
        "qae,ke->qak", grad_sv, value_self, preferred_element_type=jnp.float32
    )
    back_term, grad_gain_self = norm_backward(grad_hidden_one, normal_one, factor_one, norm_self)
    decoder_grad = grad_one + back_term
    key_part, value_part = (
        lax.psum_scatter(full_key, "pa", scatter_dimension=0, tiled=True),
        lax.psum_scatter(full_value, "pa", scatter_dimension=0, tiled=True),
    )
    summed = lax.psum(
        (
            grad_query_self,
            grad_key_self,
            grad_value_self,
            grad_out_self,
            grad_query_cross,
            key_part,
            value_part,
            grad_out_cross,
            grad_expand,
            grad_reduce,
            grad_gain_self,
            grad_gain_cross,
            grad_gain_ffn,
            grad_table,
        ),
        "pb",
    )
    key_total = summed[5]
    value_total = summed[6]
    rest_sums = (
        summed[0],
        summed[1],
        summed[2],
        summed[3],
        summed[4],
        summed[7],
        summed[8],
        summed[9],
        summed[10],
        summed[11],
        summed[12],
        summed[13],
    )
    return (
        decoder_out,
        decoder_grad,
        encoding_grad,
        rest_sums[0],
        rest_sums[1],
        rest_sums[2],
        rest_sums[3],
        rest_sums[4],
        key_total,
        value_total,
        rest_sums[5],
        rest_sums[6],
        rest_sums[7],
        rest_sums[8],
        rest_sums[9],
        rest_sums[10],
        rest_sums[11],
    )


def solution(mesh):
    placed = (
        P("pb", None, None),
        P("pb", "pa", None),
        P("pb", None, None),
        P("pb"),
        P("pb"),
        P(),
        P("pa", None),
        P("pa", None),
        P("pa", None),
        P("pa", None),
        P("pa", None),
        P("pa", None),
        P("pa", None),
        P("pa", None),
        P("pa", None),
        P("pa", None),
        P(),
        P(),
        P(),
        P(),
    )
    return jax.shard_map(
        shards,
        mesh=mesh,
        in_specs=placed,
        out_specs=(
            P("pb", None, None),
            P("pb", None, None),
            P("pb", "pa", None),
            P("pa", None),
            P("pa", None),
            P("pa", None),
            P("pa", None),
            P("pa", None),
            P("pa", None),
            P("pa", None),
            P("pa", None),
            P("pa", None),
            P("pa", None),
            P(),
            P(),
            P(),
            P(),
        ),
        check_vma=False,
    )
```

profile of v0, /device:TPU:1, one launch (start us, length us, event | category | flops | bytes accessed | tf_op | source)
XLA Modules:
  0.0 588.7 jit_solution(12000666798541889678)
XLA Ops:
  25.2 88.3 %all-gather.4.cloned.1.call-done = bf16[8,768,768]{2,1,0:T(8,128)(2,1)} async-done(((bf16[8,96,768]{2,1,0:T(8,128)(2,1)}), bf16[8,768,768]{2,1,0:T(8,128)(2,1)}) %all-gather.4.cloned.1.call-update) | async-done | bytes 9437200 | tf_op jit(solution)/shard_map/all_gather | solution.py:68
  141.2 4.3 convolution_convert_fusion.1
  148.1 22.3 %pmax.7 = f32[4,12,20]{2,1,0:T(8,128)S(1)} all-reduce(f32[4,12,20]{2,1,0:T(8,128)S(1)} %get-tuple-element.128), channel_id=1, replica_groups=mesh['pb'=4,'pa'=8] {'pa'}, use_global_device_ids=true, to_apply=%region_5.6 | all-reduce | flops 960 | bytes 7680 | tf_op jit(solution)/shard_map/pmax | solution.py:135
  170.4 4.3 convolution_convert_fusion.2
  182.7 26.8 %psum.120 = f32[4,12,20]{2,1,0:T(8,128)S(1)} all-reduce(f32[4,12,20]{2,1,0:T(8,128)S(1)} %fusion.14), channel_id=1, replica_groups=mesh['pb'=4,'pa'=8] {'pa'}, use_global_device_ids=true, to_apply=%region_8.9 | all-reduce | flops 960 | bytes 7680 | tf_op jit(solution)/shard_map/psum | solution.py:141
  209.5 25.7 %all-reduce.6.cloned.1.call-done = f32[4,20,12,64]{3,1,2,0:T(8,128)} async-done(((f32[4,20,12,64]{3,1,2,0:T(8,128)}), f32[4,20,12,64]{3,1,2,0:T(8,128)}) %all-reduce.6.cloned.1.call-update) | async-done | bytes 245776 | tf_op jit(solution)/shard_map/psum | solution.py:141
  240.0 49.7 %all-gather.6.cloned.1.call-done = bf16[768,3072]{1,0:T(8,128)(2,1)} async-done(((bf16[96,3072]{1,0:T(8,128)(2,1)}), bf16[768,3072]{1,0:T(8,128)(2,1)}) %all-gather.6.cloned.1.call-update) | async-done | bytes 4718608 | tf_op jit(solution)/shard_map/all_gather | solution.py:69
  289.8 4.8 multiply_convert_fusion.2
  294.5 47.3 %all-gather.8.cloned.1.call-done = bf16[3072,768]{1,0:T(8,128)(2,1)} async-done(((bf16[384,768]{1,0:T(8,128)(2,1)}), bf16[3072,768]{1,0:T(8,128)(2,1)}) %all-gather.8.cloned.1.call-update) | async-done | bytes 4718608 | tf_op jit(solution)/shard_map/all_gather | solution.py:70
  341.8 4.5 fusion.24
  349.4 2.5 fusion.32
  353.9 3.5 convolution_convert_fusion
  359.0 4.0 convolution_bitcast_fusion.1
  363.0 3.1 copy.305
  367.9 3.8 multiply_convert_fusion.1
  374.4 4.0 convolution_bitcast_fusion.2
  378.4 3.3 copy.303
  384.3 32.1 %all-reduce.9 = bf16[4,20,12,64]{3,0,2,1:T(4,128)(2,1)S(1)} all-reduce(f32[4,20,12,64]{3,0,2,1:T(4,128)S(1)} %bitcast.193), channel_id=1, replica_groups=mesh['pb'=4,'pa'=8] {'pa'}, use_global_device_ids=true, to_apply=%region_12.13 | all-reduce | flops 61440 | bytes 368640 | tf_op jit(solution)/shard_map/psum | solution.py:178
  451.9 4.1 fusion.29
  457.1 15.3 %all-reduce = (f32[768]{0:T(1024)}, f32[768]{0:T(1024)}, f32[768]{0:T(1024)}, f32[32,12]{0,1:T(8,128)}) all-reduce(f32[768]{0:T(1024)S(1)} %get-tuple-element.106, f32[768]{0:T(1024)S(1)} %get-tuple-element.104, f32[768]{0:T(1024)S(1)} %copy-done.49, f32[32,12]{0,1:T(8,128)S(1)} %convolution_bitcast_fusion.12), channel_id=1, replica_groups=mesh['pb'=4,'pa'=8] {'pb'}, use_global_device_ids=true, to_apply=%region_29.30 | all-reduce | flops 2688 | bytes 21504 | tf_op jit(solution)/shard_map/psum | solution.py:245
  472.4 4.2 fusion.35
  476.6 5.9 %convolution_add_fusion = f32[4,512,768]{2,1,0:T(8,128)} fusion(f32[4,512,768]{2,1,0:T(8,128)S(1)} %fusion.35, bf16[4,512,768]{1,2,0:T(8,128)(2,1)S(1)} %bitcast.192, bf16[8,768,768]{2,1,0:T(8,128)(2,1)} %all-gather.4.cloned.1.call-done), kind=kOutput, calls=%fused_computation.14 | convolution fusion | flops 2417491968 | bytes 16908288 | tf_op jit(solution)/shard_map/qse,ke->qsk/dot_general | solution.py:191
  482.5 85.3 %all-reduce.8.cloned.1.call-done = (f32[96,768]{1,0:T(8,128)}, f32[96,768]{1,0:T(8,128)}, f32[96,768]{1,0:T(8,128)}, f32[96,768]{1,0:T(8,128)}, f32[96,768]{1,0:...) async-done(((f32[96,768]{1,0:T(8,128)}, f32[96,768]{1,0:T(8,128)}, f32[96,768]{1,0:T(8,128)}, ...) | async-done | bytes 4718608 | tf_op jit(solution)/shard_map/psum | solution.py:245
  577.9 2.7 copy.411
  (230 shorter events, 121.6 us)
Async XLA Ops:
  7.2 134.0 %copy-start = (bf16[4,512,768]{2,1,0:T(8,128)(2,1)S(1)}, bf16[4,512,768]{2,1,0:T(8,128)(2,1)}, u32[]{:S(2)}) copy-start(bf16[4,512,768]{2,1,0:T(8,128)(2,1)} %param.21) | copy-start | bytes 9437188
  7.2 13.0 %copy-start.6 = (f32[4,20,768]{2,0,1:T(4,128)S(1)}, f32[4,20,768]{2,0,1:T(4,128)}, u32[]{:S(2)}) copy-start(f32[4,20,768]{2,0,1:T(4,128)} %param.20) | copy-start | bytes 737284
  7.2 13.8 %copy-start.53 = (s32[20,20]{1,0:T(8,128)S(1)}, s32[20,20]{1,0:T(8,128)}, u32[]{:S(2)}) copy-start(s32[20,20]{1,0:T(8,128)} %param.25) | copy-start | bytes 4804
  7.2 13.8 %copy-start.55 = (f32[32,12]{0,1:T(8,128)S(1)}, f32[32,12]{0,1:T(8,128)}, u32[]{:S(2)}) copy-start(f32[32,12]{0,1:T(8,128)} %param.39) | copy-start | bytes 4612
  7.2 16.3 %copy-start.51 = (s32[4]{0:T(128)S(1)}, s32[4]{0:T(128)}, u32[]{:S(2)}) copy-start(s32[4]{0:T(128)} %param.23) | copy-start | bytes 52
  7.3 16.3 %copy-start.52 = (s32[4]{0:T(128)S(1)}, s32[4]{0:T(128)}, u32[]{:S(2)}) copy-start(s32[4]{0:T(128)} %param.24) | copy-start | bytes 52
  7.3 17.2 %copy-start.46 = (f32[768]{0:T(1024)S(1)}, f32[768]{0:T(1024)}, u32[]{:S(2)}) copy-start(f32[768]{0:T(1024)} %param.36) | copy-start | bytes 9220
  7.3 106.2 %all-gather.4.cloned.1.call-start = ((), (), s32[]{:S(2)}) async-start(), calls=%async_computation.2 | async-start | bytes 10616832 | tf_op jit(solution)/shard_map/all_gather | solution.py:68
  20.1 215.1 %all-reduce.6.cloned.1.call-start = ((), (), s32[]{:S(2)}) async-start(), calls=%async_computation.3 | async-start | bytes 1179648 | tf_op jit(solution)/shard_map/psum | solution.py:141
  135.6 9.9 %copy-start.47 = (f32[4,20]{1,0:T(4,128)}, f32[4,20]{1,0:T(4,128)S(1)}, u32[]{:S(2)}) copy-start(f32[4,20]{1,0:T(4,128)S(1)} %add_rsqrt_fusion.1) | copy-start | bytes 964
  178.3 111.5 %all-gather.6.cloned.1.call-start = ((), (), s32[]{:S(2)}) async-start(), calls=%async_computation.4 | async-start | bytes 5308416 | tf_op jit(solution)/shard_map/all_gather | solution.py:69
  179.0 162.8 %all-gather.8.cloned.1.call-start = ((), (), s32[]{:S(2)}) async-start(), calls=%async_computation.5 | async-start | bytes 5308416 | tf_op jit(solution)/shard_map/all_gather | solution.py:70
  179.6 260.2 %reduce-scatter.9.cloned.1.call-start = ((), (), s32[]{:S(2)}) async-start(), calls=%async_computation.7 | async-start | bytes 2654208
  182.6 56.6 %copy-start.45 = (f32[768]{0:T(1024)S(1)}, f32[768]{0:T(1024)}, u32[]{:S(2)}) copy-start(f32[768]{0:T(1024)} %param.38) | copy-start | bytes 9220
  366.1 75.6 %reduce-scatter.7.cloned.1.call-start = ((), (), s32[]{:S(2)}) async-start(), calls=%async_computation.6 | async-start | bytes 2654208
  381.7 186.1 %all-reduce.8.cloned.1.call-start = ((), (), s32[]{:S(2)}) async-start(), calls=%async_computation.8 | async-start | bytes 9830400 | tf_op jit(solution)/shard_map/psum | solution.py:245
  384.0 32.8 %copy-start.12 = (f32[4,20,768]{2,1,0:T(8,128)S(1)}, f32[4,20,768]{2,1,0:T(8,128)}, u32[]{:S(2)}) copy-start(f32[4,20,768]{2,1,0:T(8,128)} %copy-done.11) | copy-start | bytes 737284
  384.0 32.8 %copy-start.48 = (f32[4,20]{1,0:T(4,128)S(1)}, f32[4,20]{1,0:T(4,128)}, u32[]{:S(2)}) copy-start(f32[4,20]{1,0:T(4,128)} %copy-done.47) | copy-start | bytes 964
  384.0 32.8 %copy-start.50 = (f32[768]{0:T(1024)S(1)}, f32[768]{0:T(1024)}, u32[]{:S(2)}) copy-start(f32[768]{0:T(1024)} %param.37) | copy-start | bytes 9220
  384.0 34.8 %copy-start.10 = (f32[4,20,768]{2,1,0:T(8,128)S(1)}, f32[4,20,768]{2,1,0:T(8,128)}, u32[]{:S(2)}) copy-start(f32[4,20,768]{2,1,0:T(8,128)} %copy-done.9) | copy-start | bytes 737284
  426.3 9.0 %copy-start.14 = (bf16[4,20,3072]{2,1,0:T(8,128)(2,1)S(1)}, bf16[4,20,3072]{2,1,0:T(8,128)(2,1)}, u32[]{:S(2)}) copy-start(bf16[4,20,3072]{2,1,0:T(8,128)(2,1)} %copy-done.13) | copy-start | bytes 1474564
  426.8 10.8 %copy-start.44 = (bf16[4,20,768]{2,0,1:T(4,128)(2,1)S(1)}, bf16[4,20,768]{2,0,1:T(4,128)(2,1)}, u32[]{:S(2)}) copy-start(bf16[4,20,768]{2,0,1:T(4,128)(2,1)} %convert_element_type.141) | copy-start | bytes 368644
  451.8 20.6 %copy-start.16 = (bf16[4,12,64,512]{3,2,1,0:T(8,128)(2,1)S(1)}, bf16[4,12,64,512]{3,2,1,0:T(8,128)(2,1)}, u32[]{:S(2)}) copy-start(bf16[4,12,64,512]{3,2,1,0:T(8,128)(2,1)} %copy-done.15) | copy-start | bytes 9437188
  567.8 9.4 %copy-start.37 = (f32[96,768]{1,0:T(8,128)S(1)}, f32[96,768]{1,0:T(8,128)}, u32[]{:S(2)}) copy-start(f32[96,768]{1,0:T(8,128)} %get-tuple-element.149) | copy-start | bytes 884740
  (40 other events, 131.6 us)
Sparse Core Ops, SparseCore 0:
  20.3 93.2 all-gather.3
  178.4 56.7 all-reduce.5
  236.9 52.8 all-gather.5
  291.3 50.5 all-gather.7
  366.2 34.4 reduce-scatter.8
  402.9 36.2 reduce-scatter.6
  445.7 122.1 all-reduce.7
where the time goes:
time: 599 us; the launch traced here: 589 us
  waiting for transfers between devices  298 us (50%)
  matrix products  103 us (17%)
  blocking collectives  96.5 us (16%)
  local copies, waits for them, and re-layouts  63.3 us (11%)
  between operations  15.3 us (3%)
  other arithmetic  12 us (2%)
    all_gather x1, waiting for transfers between devices, shards(): lax.all_gather(stacked, 'pa', axis=1, tiled=True)  88.3 us
    psum x1, waiting for transfers between devices, shards(): lax.psum((grad_query_self, grad_key_self, grad_value_self, grad_out_self,...  85.3 us
    all_gather x1, waiting for transfers between devices, shards(): lax.all_gather(ffn_expand, 'pa', axis=0, tiled=True)  49.7 us
    all_gather x1, waiting for transfers between devices, shards(): lax.all_gather(ffn_reduce, 'pa', axis=0, tiled=True)  47.3 us
    unnamed x140, local copies, waits for them, and re-layouts  46.2 us
    psum x1, blocking collectives, shards(): lax.psum(part_query, 'pa')  32.1 us
    dot_general x10, matrix products, product(): return jnp.dot(left, right, preferred_element_type=jnp.float32)  29.6 us
    psum x1, blocking collectives, shards(): numerator, totals = lax.psum((part_num, part_total), 'pa')  26.8 us
  transfers between devices with their start and end apart: 7, of which 5 were waited for; matrix products, arithmetic and copies ran while one was open for 14% of the time, Pallas kernels for 0%

commit v1 on v0

--- a/solution.py
+++ b/solution.py
@@ -1,6 +1,10 @@
+import types
+
 import jax
 import jax.numpy as jnp
 from jax import lax
+from jax.experimental import pallas as pl
+from jax.experimental.pallas import tpu as pltpu
 from jax.sharding import PartitionSpec as P
 
 epsilon = 1e-06
@@ -298,7 +302,7 @@
     )
 
 
-def solution(mesh):
+def generic(mesh):
     placed = (
         P("pb", None, None),
         P("pb", "pa", None),
@@ -346,3 +350,982 @@
         ),
         check_vma=False,
     )
+
+
+MESH = pl.DeviceIdType.MESH
+F32, BF = jnp.float32, jnp.bfloat16
+ANS, PAD, OWN, ALL = 20, 24, 48, 96
+WIDTH, HEADS, SIZE, PART = 768, 12, 64, 192
+ROWS = HEADS * PAD
+SLOT, FF, BUCKETS = 512, 3072, 32
+CQ, CK, CV, CO, SO, SQ, SK, SV, EX, RD, EN = range(11)
+GELU_A, GELU_B = 0.7978845608028654, 0.044715
+
+
+def nn(a, b):
+    return lax.dot_general(a, b, (((1,), (0,)), ((), ())), preferred_element_type=F32)
+
+
+def nt(a, b):
+    return lax.dot_general(a, b, (((1,), (1,)), ((), ())), preferred_element_type=F32)
+
+
+def tn(a, b):
+    return lax.dot_general(a, b, (((0,), (0,)), ((), ())), preferred_element_type=F32)
+
+
+def lanes(rows, width):
+    return lax.broadcasted_iota(jnp.int32, (rows, width), 1)
+
+
+def split4(v):
+    out = []
+    for j in range(4):
+        base = PART * j // 128 * 128
+        t = v[:, base : base + 256]
+        out.append(pltpu.roll(t, PART, 1) if PART * j != base else t)
+    return out
+
+
+def join4(parts):
+    low = lanes(parts[0].shape[0], 128) < 64
+    tiles = []
+    for a, b in ((parts[0], parts[1]), (parts[2], parts[3])):
+        b = pltpu.roll(b, 64, 1)
+        tiles += [a[:, :128], jnp.where(low, a[:, 128:], b[:, :128]), b[:, 128:]]
+    return jnp.concatenate(tiles, 1)
+
+
+def join3(parts):
+    low = lanes(parts[0].shape[0], 128) < 64
+    a, b = parts[0], pltpu.roll(parts[1], 64, 1)
+    return jnp.concatenate([a[:, :128], jnp.where(low, a[:, 128:], b[:, :128]), b[:, 128:], parts[2]], 1)
+
+
+def part3(v):
+    return [v[:, :256], pltpu.roll(v[:, 128:384], PART, 1), v[:, 384:]]
+
+
+def choose(parts, index):
+    v = parts[0]
+    for j in range(1, len(parts)):
+        v = lax.select(index == j, parts[j], v)
+    return v
+
+
+def stack_heads(v, count):
+    head = lanes(*v.shape) // SIZE
+    return jnp.concatenate([jnp.where(head == h, v, 0.0) for h in range(count)], 0)
+
+
+def pick_heads(v, count):
+    head = lanes(PAD, v.shape[1]) // SIZE
+    out = jnp.zeros((PAD, v.shape[1]), F32)
+    for h in range(count):
+        out = out + jnp.where(head == h, v[PAD * h : PAD * (h + 1)], 0.0)
+    return out
+
+
+def pair_stack(v, p):
+    t = v[:, 128 * p : 128 * (p + 1)]
+    low = lanes(PAD, 128) < SIZE
+    return jnp.concatenate([jnp.where(low, t, 0.0), jnp.where(low, 0.0, t)], 0)
+
+
+SCRATCH = dict(
+    sq=((8, WIDTH, WIDTH), BF),
+    ex=((WIDTH, FF), BF),
+    rd=((WIDTH, WIDTH), BF),
+    enc=((4, SLOT, WIDTH), BF),
+    xs=((OWN, WIDTH), F32),
+    ogs=((OWN, WIDTH), F32),
+    bks=((PAD, PAD), jnp.int32),
+    bias=((3 * PAD, PAD), F32),
+    s1=((4, OWN, 640), BF),
+    r1=((3, OWN, 640), BF),
+    gact=((4, OWN, WIDTH), BF),
+    s2=((4, OWN, 256), BF),
+    r2=((3, OWN, 256), BF),
+    ag2=((8, OWN, 256), BF),
+    x6=((6, 192, 128), BF),
+    y6=((6, 192, 128), BF),
+    qk=((4, ROWS, WIDTH), BF),
+    gv=((4, ROWS, WIDTH), BF),
+    bs=((4, ROWS, WIDTH), BF),
+    as_=((4, ROWS, WIDTH), BF),
+    es=((4, ROWS, SLOT), BF),
+    gs=((4, ROWS, SLOT), BF),
+    stat=((384, 128), F32),
+    stg=((8, 8, 384), F32),
+    wrow=((128, 384), F32),
+    wcol=((384, 128), F32),
+    s5=((2, 4, OWN, 256), BF),
+    r5=((8, OWN, 256), BF),
+    mixg=((2, 4, OWN, 256), BF),
+    gm=((2, OWN, WIDTH), BF),
+    s7=((2, 4, OWN, 256), BF),
+    r7=((8, OWN, 256), BF),
+    gcq=((4, OWN, 256), BF),
+    s8=((4, OWN, 256), BF),
+    r8=((3, OWN, 256), BF),
+    dog=((8, OWN, 256), BF),
+    dgr=((2, OWN, WIDTH), F32),
+    tot=((ROWS, 128), F32),
+    gsg=((4, OWN, 640), BF),
+    tg=((4, OWN, 256), BF),
+    stz=((4, BUCKETS, 128), F32),
+    wg=((8, 96, WIDTH), BF),
+    gexs=((96, FF), BF),
+    gres=((384, WIDTH), BF),
+    p1=((2, 4, OWN, WIDTH), BF),
+    p2=((2, 4, OWN, 4096), BF),
+    p3=((2, 4, OWN, 1024), BF),
+    p4=((2, 4, OWN, 1024), BF),
+    p5=((2, 4, OWN, 1024), BF),
+    p6=((2, 4, OWN, 2560), BF),
+    sgain=((2, 4, 8, WIDTH), F32),
+    stab=((2, 4, BUCKETS, 128), F32),
+    kw1=((WIDTH, WIDTH), BF),
+    kr1=((384, WIDTH), BF),
+    kw2=((4, 96, WIDTH), BF),
+    kr2=((3, 96, WIDTH), BF),
+    kw3=((4, 96, 256), BF),
+    kr3=((3, 96, 256), BF),
+    kw4=((2, 4, 96, 256), BF),
+    vw1=((WIDTH, WIDTH), BF),
+    vr1=((384, WIDTH), BF),
+    vw2=((4, 96, WIDTH), BF),
+    vr2=((3, 96, WIDTH), BF),
+    vw3=((4, 96, 256), BF),
+    vr3=((3, 96, 256), BF),
+    vw4=((2, 4, 96, 256), BF),
+    eg=((4, SLOT, WIDTH), BF),
+)
+SEMAPHORES = 512
+NEAR, SCALAR, FAR = pltpu.VMEM, pltpu.SMEM, pl.ANY
+IN_KIND = dict(
+    x=NEAR, og=NEAR, plen=SCALAR, pcount=SCALAR, buckets=NEAR, table=SCALAR,
+    g1=NEAR, g2=NEAR, g3=NEAR, enc_h=FAR,
+    wq=FAR, wk=FAR, wv=FAR, wo=FAR, wcq=FAR, wck=FAR, wcv=FAR, wco=FAR, wex=FAR, wre=FAR,
+)
+OUT_KIND = dict(
+    decoder_out=NEAR, decoder_grad=NEAR, encoding_grad=FAR, squares=FAR, gex=FAR, gre=FAR, gains=NEAR, table_grad=NEAR,
+)
+
+
+class Wire:
+    def __init__(self, sems):
+        self.sems, self.count, self.sent = sems, 0, []
+        self.pb, self.pa = lax.axis_index("pb"), lax.axis_index("pa")
+        self.z, self.c = self.pa // 2, lax.rem(self.pa, 2)
+
+    def next(self):
+        self.count += 1
+        return self.sems.at[self.count - 1]
+
+    def local(self, src, dst):
+        copy = pltpu.make_async_copy(src, dst, self.next())
+        copy.start()
+        return copy
+
+    def remote(self, src, dst, pb, pa):
+        copy = pltpu.make_async_remote_copy(
+            src_ref=src,
+            dst_ref=dst,
+            send_sem=self.next(),
+            recv_sem=self.next(),
+            device_id=(pb, pa),
+            device_id_type=MESH,
+        )
+        copy.start()
+        self.sent.append(copy)
+        return copy
+
+    def zpeer(self, j):
+        return lax.rem(self.z + j, 4)
+
+    def ppeer(self, j):
+        return lax.rem(self.pb + j, 4)
+
+    def xside(self):
+        return self.pb + 1 - 2 * lax.rem(self.pb, 2)
+
+    def yside(self):
+        return lax.rem(self.pb + 2, 4)
+
+    def to_core(self, src, dst):
+        return self.remote(src, dst, self.pb, self.pa + 1 - 2 * self.c)
+
+    def to_z(self, src_of, dst_of):
+        out = []
+        for j in (1, 2, 3):
+            t = self.zpeer(j)
+            out.append(self.remote(src_of(t), dst_of(j), self.pb, 2 * t + self.c))
+        return out
+
+    def to_column(self, src_of, dst_of):
+        out = []
+        for j in range(1, 8):
+            t = lax.rem(self.pa + j, 8)
+            out.append(self.remote(src_of(t), dst_of(j), self.pb, t))
+        return out
+
+    def to_plane(self, src_of, dst_of):
+        out = []
+        for j in (1, 2, 3):
+            t = self.ppeer(j)
+            out.append(self.remote(src_of(t), dst_of(j), t, self.pa))
+        return out
+
+
+def received(copies):
+    for copy in copies:
+        copy.wait_recv()
+
+
+class PairGather:
+    def __init__(self, wire, sq, pair):
+        self.w, self.sq, self.pair = wire, sq, pair
+
+    def part(self, z, pb, begin, size):
+        row = pl.multiple_of(96 * (2 * z + self.w.c) + 48 * lax.rem(pb, 2), 16)
+        return self.sq.at[2 * self.pair + pb // 2, pl.ds(row, 48), pl.ds(begin, size)]
+
+    def start(self):
+        w = self.w
+        src = self.part(w.z, w.pb, 0, WIDTH)
+        self.a = w.to_z(lambda t: src, lambda j: src)
+
+    def plane(self):
+        w = self.w
+        received(self.a)
+        self.b = []
+        for i in (1, 2, 3):
+            ref = self.part(w.zpeer(i), w.pb, 0, WIDTH)
+            self.b += [w.remote(ref, ref, side, w.pa) for side in (w.xside(), w.yside())]
+
+    def relay(self):
+        w = self.w
+        received(self.b)
+        self.d = []
+        for i in (1, 2, 3):
+            ref = self.part(w.zpeer(i), w.xside(), 0, WIDTH // 2)
+            self.d.append(w.remote(ref, ref, w.yside(), w.pa))
+            ref = self.part(w.zpeer(i), w.yside(), WIDTH // 2, WIDTH // 2)
+            self.d.append(w.remote(ref, ref, w.xside(), w.pa))
+
+    def core(self):
+        w = self.w
+        received(self.d)
+        self.e = []
+        for k in (0, 1):
+            for i in (1, 2, 3):
+                row = pl.multiple_of(96 * (2 * w.zpeer(i) + w.c), 16)
+                ref = self.sq.at[2 * self.pair + k, pl.ds(row, 96), :]
+                self.e.append(w.to_core(ref, ref))
+
+    def finish(self):
+        received(self.e)
+
+
+class WideGather:
+    def __init__(self, wire, ex):
+        self.w, self.ex = wire, ex
+
+    def part(self, z, pb, begin, size):
+        row = pl.multiple_of(96 * (2 * z + self.w.c), 16)
+        lane = pl.multiple_of(WIDTH * pb + begin, 128)
+        return self.ex.at[pl.ds(row, 96), pl.ds(lane, size)]
+
+    start, plane, relay = PairGather.start, PairGather.plane, PairGather.relay
+
+    def core(self):
+        w = self.w
+        received(self.d)
+        self.e = []
+        for i in (1, 2, 3):
+            ref = self.ex.at[pl.ds(pl.multiple_of(96 * (2 * w.zpeer(i) + w.c), 16), 96), :]
+            self.e.append(w.to_core(ref, ref))
+
+    finish = PairGather.finish
+
+
+class PlaneRows:
+    def __init__(self, wire, ref):
+        self.w, self.ref = w, ref = wire, ref
+        src = ref.at[w.c, w.pb]
+        self.a = [w.remote(src, src, side, w.pa) for side in (w.xside(), w.yside())]
+
+    def relay(self):
+        w = self.w
+        received(self.a)
+        half = self.ref.shape[3] // 2
+        self.a = []
+        for k, side, out in ((0, w.xside(), w.yside()), (1, w.yside(), w.xside())):
+            src = self.ref.at[w.c, side, :, pl.ds(half * k, half)]
+            self.a.append(w.remote(src, src, out, w.pa))
+
+    def core(self):
+        received(self.a)
+        src = self.ref.at[self.w.c]
+        self.b = [self.w.to_core(src, src)]
+
+    def finish(self):
+        received(self.b)
+
+
+class PlaneSmall(PlaneRows):
+    def __init__(self, wire, ref):
+        self.w, self.ref = wire, ref
+        src = ref.at[wire.c, wire.pb]
+        self.a = wire.to_plane(lambda t: src, lambda j: src)
+
+
+class CrossReduce:
+    def __init__(self, wire, refs):
+        self.w, self.refs = wire, refs
+
+    def core(self):
+        w, (w1, r1, w2, r2, w3, r3, w4) = self.w, self.refs
+        row = pl.multiple_of(384 * (1 - w.c), 16)
+        self.a = w.to_core(w1.at[pl.ds(row, 384), :], r1)
+
+    def plane(self):
+        w, (w1, r1, w2, r2, w3, r3, w4) = self.w, self.refs
+        self.a.wait_recv()
+        for k in range(4):
+            row = pl.multiple_of(384 * w.c + 96 * k, 16)
+            t = w1[pl.ds(row, 96), :].astype(F32) + r1[96 * k : 96 * (k + 1), :].astype(F32)
+            w2[k] = lowered(t)
+        self.b = w.to_plane(lambda t: w2.at[t], lambda j: r2.at[j - 1])
+
+    def line(self):
+        w, (w1, r1, w2, r2, w3, r3, w4) = self.w, self.refs
+        received(self.b)
+        t = w2[w.pb].astype(F32)
+        for j in range(3):
+            t = t + r2[j].astype(F32)
+        for j, part in enumerate(split4(t)):
+            w3[j] = lowered(part)
+        self.d = w.to_z(lambda t: w3.at[t], lambda j: r3.at[j - 1])
+
+    def spread(self):
+        w, (w1, r1, w2, r2, w3, r3, w4) = self.w, self.refs
+        received(self.d)
+        t = w3[w.z].astype(F32)
+        for j in range(3):
+            t = t + r3[j].astype(F32)
+        w4[w.c, w.pb] = lowered(t)
+        self.rows = PlaneRows(w, w4)
+
+    def result(self):
+        w4 = self.refs[-1]
+        t = w4[...].astype(F32).reshape(WIDTH, 256)
+        t = lax.select(self.w.c == 1, pltpu.roll(t, 160, 1), t)[:, :128]
+        return lowered(t.T[:96])
+
+
+def inputs_half(a, c):
+    t = a.astype(F32).reshape(384, 256)
+    t = lax.select(c == 1, pltpu.roll(t, 160, 1), t)[:, :128]
+    return lowered(t.T)
+
+
+def layer(*refs):
+    names = (*IN_KIND, *OUT_KIND)
+    r = types.SimpleNamespace(**dict(zip(names, refs)))
+    s = types.SimpleNamespace(**dict(zip(SCRATCH, refs[len(names) :])))
+    w = Wire(refs[-1])
+    pb, pa, z, c = w.pb, w.pa, w.z, w.c
+    sq, ex, rd, enc = s.sq, s.ex, s.rd, s.enc
+
+    barrier = pltpu.get_barrier_semaphore()
+    for j in range(1, 8):
+        pl.semaphore_signal(
+            barrier, inc=1, device_id=(pb, lax.rem(pa + j, 8)), device_id_type=MESH
+        )
+    for j in (1, 2, 3):
+        pl.semaphore_signal(barrier, inc=1, device_id=(w.ppeer(j), pa), device_id_type=MESH)
+
+    squares = [r.wcq, r.wck, r.wcv, r.wco, r.wo, r.wq, r.wk, r.wv]
+    own_rows = pl.ds(pl.multiple_of(96 * pa, 16), 96)
+    red_rows = pl.ds(pl.multiple_of(384 * c, 16), 384)
+    order = (SQ, SK, SV, CQ, CK, SO, CV, CO)
+    held = {i: w.local(squares[i], sq.at[i, own_rows, :]) for i in order}
+    held[EX] = w.local(r.wex, ex.at[own_rows, :])
+    held[RD] = w.local(r.wre, rd.at[red_rows, :])
+    held[EN] = w.local(r.enc_h, enc)
+
+    for dst, src in ((s.xs, r.x), (s.ogs, r.og)):
+        dst[...] = jnp.zeros((OWN, WIDTH), F32)
+        for k in (0, 1):
+            dst[PAD * k : PAD * k + ANS, :] = lax.select(c == 1, src[:, 2 + k, :], src[:, k, :])
+    s.bks[...] = jnp.zeros((PAD, PAD), jnp.int32)
+    s.bks[:ANS, :ANS] = r.buckets[...]
+    g1, g2, g3 = [ref[...].reshape(1, WIDTH) for ref in (r.g1, r.g2, r.g3)]
+    x = s.xs[...]
+    rs1 = lax.rsqrt(jnp.mean(x * x, -1, keepdims=True) + epsilon)
+    h1z = choose(split4(x * rs1 * g1), z)
+    xz = choose(split4(x), z)
+    h1b = lowered(h1z)
+    s.p6[c, pb, :, 2304:2560] = h1b
+    s.p1[c, pb] = lowered(s.ogs[...])
+
+    pl.semaphore_wait(barrier, 10)
+    other = {}
+    for i in order:
+        other[i] = w.to_core(squares[i], sq.at[i, own_rows, :])
+    other[RD] = w.to_core(r.wre, rd.at[red_rows, :])
+    other[EX] = w.to_core(r.wex, ex.at[own_rows, :])
+    gather_a, gather_b, gather_c = PairGather(w, sq, 0), PairGather(w, sq, 1), WideGather(w, ex)
+
+    def chip(i):
+        return sq[i, pl.ds(pl.multiple_of(PART * z, 16), PART), :]
+
+    parts = []
+    for i in (SQ, SK, SV):
+        held[i].wait()
+        other[i].wait_recv()
+        parts.append(split4(nn(h1b[:, :PART], chip(i))))
+    blocks = [join3([parts[k][j] for k in range(3)]) for j in range(4)]
+    for j in range(4):
+        s.s1[j] = lowered(blocks[j])
+    own_qkv = choose(blocks, z)
+    f1 = w.to_z(lambda t: s.s1.at[t], lambda j: s.r1.at[j - 1])
+    held[CQ].wait()
+    held[CK].wait()
+    gather_a.start()
+    held[CV].wait()
+    held[CO].wait()
+    gather_b.start()
+
+    bucket = s.bks[...]
+
+    def bias_head(h, carry):
+        v = jnp.zeros((PAD, PAD), F32)
+        for b in range(BUCKETS):
+            v = jnp.where(bucket == b, r.table[3 * z + h, b], v)
+        s.bias[pl.ds(pl.multiple_of(PAD * h, 8), PAD), :] = v
+        return carry
+
+    lax.fori_loop(0, 3, bias_head, 0)
+    held[RD].wait()
+    other[RD].wait_recv()
+    s.gact[z] = lowered(nt(s.p1[c, pb], rd[...]))
+
+    received(f1)
+    v = own_qkv
+    for j in range(3):
+        v = v + s.r1[j].astype(F32)
+    q3, k3, v3 = [lowered(t).astype(F32)[:, :PART] for t in part3(v)]
+
+    def attend(stacked, keys, bias):
+        i = lax.broadcasted_iota(jnp.int32, (PAD, PAD), 0)
+        j = lax.broadcasted_iota(jnp.int32, (PAD, PAD), 1)
+        seen = jnp.concatenate([(j <= i).astype(F32)] * 3, 0) > 0.5
+        t = jnp.where(seen, nt(lowered(stacked), lowered(keys)) + bias, masked_score)
+        t = jnp.exp(t - jnp.max(t, -1, keepdims=True))
+        return t / jnp.sum(t, -1, keepdims=True)
+
+    mixes, probs, stacks = [], [], []
+    for k in (0, 1):
+        rows = slice(PAD * k, PAD * (k + 1))
+        stacks.append(stack_heads(q3[rows] * 0.125, 3))
+        probs.append(attend(stacks[k], k3[rows], s.bias[...]))
+        mixes.append(pick_heads(nn(lowered(probs[k]), lowered(v3[rows])), 3))
+    mixb = lowered(jnp.concatenate(mixes, 0))
+    s.p5[c, pb, :, 768:960] = mixb
+    held[SO].wait()
+    other[SO].wait_recv()
+    parts = split4(nn(mixb, chip(SO)))
+    for j in range(4):
+        s.s2[j] = lowered(parts[j])
+    own_o = choose(parts, z)
+    f2 = w.to_z(lambda t: s.s2.at[t], lambda j: s.r2.at[j - 1])
+    gather_a.plane()
+
+    received(f2)
+    r1z = xz + own_o
+    for j in range(3):
+        r1z = r1z + s.r2[j].astype(F32)
+    counts = lanes(OWN, 256) < PART
+    g2z = choose(split4(jnp.broadcast_to(g2, (OWN, WIDTH))), z)
+    square = jnp.sum(jnp.where(counts, r1z * r1z, 0.0), -1, keepdims=True)
+    high = lowered(square).astype(F32)
+    tail = jnp.where(lanes(OWN, 256) < 224, high, square - high)
+    s.ag2[pa] = lowered(jnp.where(counts, r1z * g2z, tail))
+    f3 = w.to_column(lambda t: s.ag2.at[pa], lambda j: s.ag2.at[pa])
+    gather_b.plane()
+    held[EX].wait()
+    gather_c.start()
+    gather_a.relay()
+    gather_a.core()
+
+    received(f3)
+    blocks = [[s.ag2[2 * j + k].astype(F32) for j in range(4)] for k in (0, 1)]
+    rs2 = []
+    for k in (0, 1):
+        t = blocks[k][0] + blocks[k][1] + blocks[k][2] + blocks[k][3]
+        lane = lanes(OWN, 256)
+        t = jnp.sum(jnp.where((lane == 192) | (lane == 224), t, 0.0), -1, keepdims=True)
+        rs2.append(lax.rsqrt(t * (1.0 / WIDTH) + epsilon))
+    gather_b.relay()
+    gather_a.finish()
+    other[CQ].wait_recv()
+    cq = jnp.zeros((ALL, WIDTH), F32)
+    for j in range(4):
+        t = jnp.concatenate([s.ag2[2 * j], s.ag2[2 * j + 1]], 0)[:, :PART]
+        cq = cq + nn(t, sq[CQ, PART * j : PART * (j + 1), :])
+    cq = cq * jnp.concatenate(rs2, 0)
+    cq = lowered(cq).astype(F32) * 0.125
+    other[CK].wait_recv()
+    for p in range(6):
+        t = jnp.concatenate([pair_stack(cq[PAD * q : PAD * (q + 1)], p) for q in range(4)], 0)
+        s.x6[p] = lowered(t)
+        t = lowered(nt(s.x6[p], sq[CK, :, 128 * p : 128 * (p + 1)]))
+        for q in range(4):
+            s.qk[q, 48 * p : 48 * (p + 1), :] = t[48 * q : 48 * (q + 1)]
+    held[EN].wait()
+    s.stat[...] = jnp.zeros((384, 128), F32)
+
+    def scores(q, carry):
+        size = r.plen[q]
+        per = lax.select(size <= SLOT // 2, 2, 1)
+        kept = jnp.minimum(jnp.maximum(r.pcount[q] - pa * per, 0), per) * size
+        valid = lanes(ROWS, SLOT) < kept
+        t = jnp.where(valid, nt(s.qk[q], enc[q]), masked_score)
+        top = jnp.max(t, -1, keepdims=True)
+        t = jnp.where(valid, jnp.exp(t - top), 0.0)
+        total = jnp.sum(t, -1, keepdims=True)
+        s.es[q] = lowered(t)
+        s.bs[q] = lowered(nn(s.es[q], enc[q]))
+        lane = lanes(ROWS, 128)
+        old = s.stat[:ROWS, :]
+        s.stat[:ROWS, :] = jnp.where(lane == q, top, jnp.where(lane == 4 + q, total, old))
+        return carry
+
+    lax.fori_loop(0, 4, scores, 0)
+    s.stg[pa] = s.stat[...].T[:8]
+    f5 = w.to_column(lambda t: s.stg.at[pa], lambda j: s.stg.at[pa])
+    gather_b.core()
+    gather_c.plane()
+    gather_b.finish()
+    other[CV].wait_recv()
+    low = lanes(PAD, 128) < SIZE
+    tiles = [[] for q in range(4)]
+    for p in range(6):
+        t = jnp.concatenate([s.bs[q, 48 * p : 48 * (p + 1), :] for q in range(4)], 0)
+        t = nn(t, sq[CV, :, 128 * p : 128 * (p + 1)])
+        for q in range(4):
+            a = t[48 * q : 48 * (q + 1)]
+            tiles[q].append(jnp.where(low, a[:PAD], a[PAD:]))
+    num = jnp.concatenate([jnp.concatenate(tiles[q], 1) for q in range(4)], 0)
+    for k in (0, 1):
+        for j, part in enumerate(split4(num[OWN * k : OWN * (k + 1)])):
+            s.s5[k, j] = lowered(part)
+    f5 += w.to_column(lambda t: s.s5.at[lax.rem(t, 2), t // 2], lambda j: s.r5.at[pa])
+    s.r5[pa] = s.s5[c, z]
+    gact_copies = w.to_z(lambda t: s.gact.at[z], lambda j: s.gact.at[z])
+    rows1 = PlaneRows(w, s.p1)
+    r1full = join4(blocks_of(s.ag2, c)) / g2
+    rs2o = lax.select(c == 1, rs2[1], rs2[0])
+    n2 = r1full * rs2o
+    s.p4[c, pb, :, 768:1024] = lowered(choose(split4(n2 * g2), z))
+
+    received(f5)
+    stats = [s.stg[k] for k in range(8)]
+    top = stats[0]
+    for k in range(1, 8):
+        top = jnp.maximum(top, stats[k])
+    scale = [jnp.exp(t - top) for t in stats]
+    total = jnp.zeros((8, 384), F32)
+    for k in range(8):
+        total = total + scale[k] * pltpu.roll(stats[k], 4, 0)
+    inverse = 1.0 / total
+    s.wrow[...] = jnp.zeros((128, 384), F32)
+    mine = jnp.zeros((8, 384), F32)
+    for k in range(8):
+        t = scale[k] * inverse
+        mine = lax.select(pa == k, t, mine)
+        s.wrow[2 * k : 2 * k + 2, :] = lax.select(c == 1, t[2:4], t[0:2])
+    s.wrow[16:20, :] = mine[0:4]
+    s.wcol[...] = s.wrow[...].T
+    w3 = s.wcol[pl.ds(pl.multiple_of(3 * PAD * z, 8), 3 * PAD), :]
+    lane = lanes(PAD, 256)
+    sums = [jnp.zeros((PAD, 256), F32) for k in (0, 1)]
+    for m in range(8):
+        block = s.r5[m].astype(F32)
+        for k in (0, 1):
+            col = [w3[PAD * h : PAD * (h + 1), 2 * m + k : 2 * m + k + 1] for h in range(3)]
+            t = jnp.where(lane < 64, col[0], jnp.where(lane < 128, col[1], col[2]))
+            sums[k] = sums[k] + t * block[PAD * k : PAD * (k + 1)]
+    mixc = lowered(jnp.concatenate(sums, 0))
+    s.mixg[c, z] = mixc
+    s.p3[c, pb, :, 768:1024] = mixc
+    f6 = w.to_z(lambda t: s.mixg.at[c, z], lambda j: s.mixg.at[c, z])
+    gather_c.relay()
+    gather_c.core()
+    other[CO].wait_recv()
+    received(f6)
+    mix_core = w.to_core(s.mixg.at[c], s.mixg.at[c])
+    after = jnp.zeros((OWN, WIDTH), F32)
+    for j in range(4):
+        after = after + nn(s.mixg[c, j][:, :PART], sq[CO, PART * j : PART * (j + 1), :])
+    r2z = r1z + choose(split4(after), z)
+    resid = r1full + after
+    rs3 = lax.rsqrt(jnp.mean(resid * resid, -1, keepdims=True) + epsilon)
+    n3 = resid * rs3
+    h3 = lowered(n3 * g3)
+    s.p2[c, pb, :, 3072:3328] = lowered(choose(split4(n3 * g3), z))
+    received(gact_copies)
+    gather_c.finish()
+    other[EX].wait_recv()
+    gh3 = jnp.zeros((OWN, WIDTH), F32)
+    for j in range(4):
+        cols = slice(WIDTH * j, WIDTH * (j + 1))
+        v = nn(h3, ex[:, cols])
+        t = jnp.tanh(GELU_A * (v + GELU_B * v * v * v))
+        act = lowered(0.5 * v * (1.0 + t))
+        slope = 0.5 * (1.0 + t) + 0.5 * v * (1.0 - t * t) * GELU_A * (1.0 + 3.0 * GELU_B * v * v)
+        gp = lowered(s.gact[j].astype(F32) * slope)
+        s.p2[c, pb, :, cols] = gp
+
+        @pl.when(z == j)
+        def keep():
+            s.p2[c, pb, :, 3328:4096] = act
+
+        gh3 = gh3 + nt(gp, ex[:, cols])
+    og = s.ogs[...]
+    gain3 = jnp.sum(gh3 * n3, 0, keepdims=True)
+    t = gh3 * g3
+    grad_two = og + rs3 * (t - n3 * jnp.mean(t * n3, -1, keepdims=True))
+    gcb = lowered(grad_two)
+    s.p3[c, pb, :, :768] = gcb
+    s.gm[c] = lowered(nt(gcb, sq[CO]))
+    f7 = w.to_core(s.gm.at[c], s.gm.at[c])
+    rows1.relay()
+    rows3 = PlaneRows(w, s.p3)
+    rows2 = PlaneRows(w, s.p2)
+    mix_core.wait_recv()
+    f7.wait_recv()
+
+    gms = [s.gm[k].astype(F32) for k in (0, 1)]
+    mxs = [join4([s.mixg[k, j].astype(F32) for j in range(4)]) for k in (0, 1)]
+    gm_q = [gms[q // 2][PAD * (q % 2) : PAD * (q % 2 + 1)] for q in range(4)]
+    mx_q = [mxs[q // 2][PAD * (q % 2) : PAD * (q % 2 + 1)] for q in range(4)]
+    tots = [[] for q in range(4)]
+    for p in range(6):
+        blocks_p = []
+        for q in range(4):
+            col = s.wcol[48 * p : 48 * (p + 1), 16 + q : 17 + q]
+            y = pair_stack(gm_q[q], p) * col
+            m = mx_q[q][:, 128 * p : 128 * (p + 1)]
+            tots[q].append(-jnp.sum(y * jnp.concatenate([m, m], 0), -1, keepdims=True))
+            blocks_p.append(y)
+        s.y6[p] = lowered(jnp.concatenate(blocks_p, 0))
+        t = lowered(nt(s.y6[p], sq[CV, :, 128 * p : 128 * (p + 1)]))
+        for q in range(4):
+            s.gv[q, 48 * p : 48 * (p + 1), :] = t[48 * q : 48 * (q + 1)]
+    lane = lanes(ROWS, 128)
+    t = jnp.zeros((ROWS, 128), F32)
+    for q in range(4):
+        t = jnp.where(lane == q, jnp.concatenate(tots[q], 0), t)
+    s.tot[...] = t
+    for p in range(6):
+        t = jnp.concatenate([s.bs[q, 48 * p : 48 * (p + 1), :] for q in range(4)], 0)
+        s.vw1[128 * p : 128 * (p + 1), :] = lowered(tn(s.y6[p], t))
+    vred = CrossReduce(w, [s.vw1, s.vr1, s.vw2, s.vr2, s.vw3, s.vr3, s.vw4])
+    vred.core()
+
+    def grads(q, carry):
+        pick = lanes(ROWS, 128) == q
+        tot = jnp.sum(jnp.where(pick, s.tot[...], 0.0), -1, keepdims=True)
+        t = nt(s.gv[q], enc[q]) + tot
+        s.gs[q] = lowered(s.es[q].astype(F32) * t)
+        s.as_[q] = lowered(nn(s.gs[q], enc[q]))
+        return carry
+
+    lax.fori_loop(0, 4, grads, 0)
+    tiles = [[] for q in range(4)]
+    for p in range(6):
+        t = jnp.concatenate([s.as_[q, 48 * p : 48 * (p + 1), :] for q in range(4)], 0)
+        t = nn(t, sq[CK, :, 128 * p : 128 * (p + 1)])
+        for q in range(4):
+            a = t[48 * q : 48 * (q + 1)]
+            tiles[q].append(jnp.where(low, a[:PAD], a[PAD:]))
+    num = jnp.concatenate([jnp.concatenate(tiles[q], 1) for q in range(4)], 0) * 0.125
+    for k in (0, 1):
+        for j, part in enumerate(split4(num[OWN * k : OWN * (k + 1)])):
+            s.s7[k, j] = lowered(part)
+    f8 = w.to_column(lambda t: s.s7.at[lax.rem(t, 2), t // 2], lambda j: s.r7.at[pa])
+    s.r7[pa] = s.s7[c, z]
+    vred.plane()
+    for p in range(6):
+        t = jnp.concatenate([s.as_[q, 48 * p : 48 * (p + 1), :] for q in range(4)], 0)
+        s.kw1[128 * p : 128 * (p + 1), :] = lowered(tn(s.x6[p], t))
+    kred = CrossReduce(w, [s.kw1, s.kr1, s.kw2, s.kr2, s.kw3, s.kr3, s.kw4])
+    kred.core()
+    rows3.relay()
+    rows2.relay()
+    rows1.core()
+    out_copies = []
+
+    def encoding_grad(q):
+        s.eg[q] = lowered(tn(s.es[q], s.gv[q]) + tn(s.gs[q], s.qk[q]))
+        out_copies.append(w.local(s.eg.at[q], r.encoding_grad.at[q]))
+
+    encoding_grad(0)
+    encoding_grad(1)
+
+    received(f8)
+    t = s.r7[0].astype(F32)
+    for k in range(1, 8):
+        t = t + s.r7[k].astype(F32)
+    s.gcq[z] = lowered(t)
+    f9 = w.to_z(lambda t: s.gcq.at[z], lambda j: s.gcq.at[z])
+    kred.plane()
+    rows3.core()
+    parts = split4(nn(s.p2[c, pb, :, 3328:4096], rd[...]))
+    for j in range(4):
+        s.s8[j] = lowered(parts[j])
+    own_d = choose(parts, z)
+    fo = w.to_z(lambda t: s.s8.at[t], lambda j: s.r8.at[j - 1])
+    encoding_grad(2)
+    encoding_grad(3)
+
+    received(f9)
+    gcq = lowered(join4([s.gcq[j].astype(F32) for j in range(4)]))
+    s.p4[c, pb, :, :768] = gcq
+    rows4 = PlaneRows(w, s.p4)
+    gh2 = nt(gcq, sq[CQ])
+    gain2 = jnp.sum(gh2 * n2, 0, keepdims=True)
+    t = gh2 * g2
+    grad_one = grad_two + rs2o * (t - n2 * jnp.mean(t * n2, -1, keepdims=True))
+    gab = lowered(grad_one)
+    s.p5[c, pb, :, :768] = gab
+    rows5 = PlaneRows(w, s.p5)
+    gsm = lowered(nt(gab, chip(SO))).astype(F32)
+    gsum = jnp.zeros((3 * PAD, PAD), F32)
+    dq, dk, dv = [], [], []
+    for k in (0, 1):
+        rows = slice(PAD * k, PAD * (k + 1))
+        prob = probs[k]
+        stacked = lowered(stack_heads(gsm[rows], 3))
+        gw = nt(stacked, lowered(v3[rows]))
+        gsb = lowered(prob * (gw - jnp.sum(gw * prob, -1, keepdims=True)))
+        gsum = gsum + gsb.astype(F32)
+        dq.append(pick_heads(nn(gsb, lowered(k3[rows])), 3) * 0.125)
+        dk.append(tn(gsb, lowered(stacks[k])))
+        dv.append(tn(lowered(prob), stacked))
+    gap = jnp.zeros((OWN, 64), F32)
+    three = [jnp.concatenate([jnp.concatenate(t, 0), gap], 1) for t in (dq, dk, dv)]
+    s.gsg[z] = lowered(join3(three))
+    f10 = w.to_z(lambda t: s.gsg.at[z], lambda j: s.gsg.at[z])
+    s.bias[...] = gsum
+
+    def table_head(h, carry):
+        v = s.bias[pl.ds(pl.multiple_of(PAD * h, 8), PAD), :]
+        rows = [jnp.sum(jnp.where(bucket == b, v, 0.0), 0, keepdims=True) for b in range(BUCKETS)]
+        col = jnp.sum(jnp.concatenate(rows, 0), -1, keepdims=True)
+        return jnp.where(lanes(BUCKETS, 128) == 3 * z + h, col, carry)
+
+    s.stz[z] = lax.fori_loop(0, 3, table_head, jnp.zeros((BUCKETS, 128), F32))
+    ft = w.to_z(lambda t: s.stz.at[z], lambda j: s.stz.at[z])
+    rows2.core()
+    vred.line()
+    received(fo)
+    t = r2z + own_d
+    for j in range(3):
+        t = t + s.r8[j].astype(F32)
+    s.dog[pa] = lowered(t)
+    fg = w.to_column(lambda t: s.dog.at[pa], lambda j: s.dog.at[pa])
+    rows1.finish()
+
+    def half_product(ref, begin, index, rows):
+        rows.finish()
+        lhs = inputs_half(ref[:, :, :, begin : begin + 256], c)
+        s.wg[index] = lowered(nn(lhs, ref[:, :, :, :768].reshape(384, WIDTH))[:96])
+        out_copies.append(w.local(s.wg.at[index], r.squares.at[index]))
+
+    half_product(s.p3, 768, 7, rows3)
+
+    received(f10)
+    unpacked = [part3(s.gsg[j].astype(F32)) for j in range(4)]
+    three = [lowered(join4([unpacked[j][k] for j in range(4)])) for k in range(3)]
+    for k in range(3):
+        s.p6[c, pb, :, 768 * k : 768 * (k + 1)] = three[k]
+    rows6 = PlaneRows(w, s.p6)
+    gh1 = nt(three[0], chip(SQ)) + nt(three[1], chip(SK)) + nt(three[2], chip(SV))
+    g1z = choose(split4(jnp.broadcast_to(g1, (OWN, WIDTH))), z)
+    s.tg[z] = lowered(jnp.concatenate([gh1 * g1z[:, :PART], gap], 1))
+    f11 = w.to_z(lambda t: s.tg.at[z], lambda j: s.tg.at[z])
+    received(ft)
+    s.stab[c, pb] = s.stz[0] + s.stz[1] + s.stz[2] + s.stz[3]
+    tab_rows = PlaneSmall(w, s.stab)
+    kred.line()
+    rows4.relay()
+    rows5.relay()
+    vred.spread()
+    rows2.finish()
+    p2 = s.p2
+    lhs = inputs_half(p2[:, :, :, 3072:3328], c)
+    for j in range(4):
+        cols = slice(WIDTH * j, WIDTH * (j + 1))
+        s.gexs[:, cols] = lowered(nn(lhs, p2[:, :, :, cols].reshape(384, WIDTH))[:96])
+    out_copies.append(w.local(s.gexs, r.gex))
+    received(f11)
+    t = join4([s.tg[j].astype(F32) for j in range(4)])
+    n1 = s.xs[...] * rs1
+    gain1 = jnp.sum(t * n1, 0, keepdims=True) / g1
+    s.dgr[c] = grad_one + rs1 * (t - n1 * jnp.mean(t * n1, -1, keepdims=True))
+    fd = w.to_core(s.dgr.at[c], s.dgr.at[c])
+    s.sgain[c, pb] = jnp.concatenate([gain1, gain2, gain3, jnp.zeros((5, WIDTH), F32)], 0)
+    gain_rows = PlaneSmall(w, s.sgain)
+    rows6.relay()
+    kred.spread()
+    vred.rows.relay()
+    rows4.core()
+    rows5.core()
+    half = pl.ds(pl.multiple_of(3328 + 384 * c, 128), 384)
+    lhs = lowered(p2[:, :, :, half].astype(F32).reshape(384, 384).T)
+    s.gres[...] = lowered(nn(lhs, s.p1[...].reshape(384, WIDTH)))
+    out_copies.append(w.local(s.gres, r.gre))
+    half_product(s.p4, 768, 4, rows4)
+    half_product(s.p5, 768, 3, rows5)
+    vred.rows.core()
+    kred.rows.relay()
+    tab_rows.core()
+    gain_rows.core()
+    received(fg)
+    fd.wait_recv()
+    for k in (0, 1):
+        t = join4([s.dog[2 * j + k].astype(F32) for j in range(4)])
+        for m in (0, 1):
+            r.decoder_out[:, 2 * k + m, :] = t[PAD * m : PAD * m + ANS]
+            r.decoder_grad[:, 2 * k + m, :] = s.dgr[k, PAD * m : PAD * m + ANS, :]
+    rows6.core()
+    kred.rows.core()
+    vred.rows.finish()
+    s.wg[6] = vred.result()
+    out_copies.append(w.local(s.wg.at[6], r.squares.at[6]))
+    gain_rows.finish()
+    tab_rows.finish()
+    t = s.sgain[0, 0]
+    u = s.stab[0, 0]
+    for k in range(1, 8):
+        t = t + s.sgain[k // 4, k % 4]
+        u = u + s.stab[k // 4, k % 4]
+    r.gains[...] = t
+    r.table_grad[...] = u
+    kred.rows.finish()
+    s.wg[5] = kred.result()
+    out_copies.append(w.local(s.wg.at[5], r.squares.at[5]))
+    rows6.finish()
+    ref = s.p6
+    lhs = inputs_half(ref[:, :, :, 2304:2560], c)
+    for k in range(3):
+        s.wg[k] = lowered(nn(lhs, ref[:, :, :, 768 * k : 768 * (k + 1)].reshape(384, WIDTH))[:96])
+        out_copies.append(w.local(s.wg.at[k], r.squares.at[k]))
+    for copy in out_copies:
+        copy.wait()
+    for copy in w.sent:
+        copy.wait_send()
+
+
+def blocks_of(ref, c):
+    return [ref[2 * j + c].astype(F32) for j in range(4)]
+
+
+def write(dout, dgrad, eg, sq, gex, gre, gains, table, *refs):
+    outs, (veg, vsq, vex, vre, weg, wsq, wex, wre, sems) = refs[:17], refs[17:]
+    o_out, o_grad, o_eg, outs = outs[0], outs[1], outs[2], outs[3:]
+    jobs = [(eg.at[q], veg.at[q], weg.at[q], o_eg.at[q]) for q in range(4)]
+    jobs += [(gex, vex, wex, outs[8]), (gre, vre, wre, outs[9])]
+    jobs += [(sq.at[k], vsq.at[k], wsq.at[k], outs[k]) for k in range(8)]
+    loads = [pltpu.make_async_copy(j[0], j[1], sems.at[k]) for k, j in enumerate(jobs)]
+    for copy in loads:
+        copy.start()
+    o_out[...] = dout[...]
+    o_grad[...] = dgrad[...]
+    for k in range(3):
+        outs[10 + k][...] = gains[k : k + 1, :].reshape(WIDTH)
+    outs[13][...] = table[...].T[:HEADS]
+    stores = []
+    for k, (src, near, wide, dst) in enumerate(jobs):
+        loads[k].wait()
+        wide[...] = near[...].astype(F32)
+        stores.append(pltpu.make_async_copy(wide, dst, sems.at[len(jobs) + k]))
+        stores[-1].start()
+    for copy in stores:
+        copy.wait()
+
+
+def fused(x, enc, og, plen, pcount, buckets, wq, wk, wv, wo, wcq, wck, wcv, wco, wex, wre, g1, g2, g3, table):
+    def shape(*dims, kind=F32):
+        return jax.ShapeDtypeStruct(dims, kind)
+
+    rows = shape(ANS, 4, WIDTH)
+    mid = pl.pallas_call(
+        layer,
+        out_shape=[
+            rows,
+            rows,
+            shape(4, SLOT, WIDTH, kind=BF),
+            shape(8, 96, WIDTH, kind=BF),
+            shape(96, FF, kind=BF),
+            shape(384, WIDTH, kind=BF),
+            shape(8, WIDTH),
+            shape(BUCKETS, 128),
+        ],
+        in_specs=[pl.BlockSpec(memory_space=k) for k in IN_KIND.values()],
+        out_specs=[pl.BlockSpec(memory_space=k) for k in OUT_KIND.values()],
+        scratch_shapes=[pltpu.VMEM(*v) for v in SCRATCH.values()]
+        + [pltpu.SemaphoreType.DMA((SEMAPHORES,))],
+        compiler_params=pltpu.CompilerParams(
+            collective_id=0, has_side_effects=True, vmem_limit_bytes=62 * 2**20
+        ),
+    )(
+        jnp.transpose(x, (1, 0, 2)),
+        jnp.transpose(og, (1, 0, 2)),
+        *(plen, pcount, buckets, table.T, g1, g2, g3, enc),
+        *(wq, wk, wv, wo, wcq, wck, wcv, wco, wex, wre),
+    )
+    near, far = pl.BlockSpec(memory_space=NEAR), pl.BlockSpec(memory_space=FAR)
+    square = shape(96, WIDTH)
+    out = pl.pallas_call(
+        write,
+        out_shape=[
+            *(rows, rows, shape(4, SLOT, WIDTH)),
+            *[square] * 8,
+            *(shape(96, FF), shape(384, WIDTH)),
+            *[shape(WIDTH)] * 3,
+            shape(HEADS, BUCKETS),
+        ],
+        in_specs=[near, near, far, far, far, far, near, near],
+        out_specs=[near, near, far, *[far] * 10, *[near] * 4],
+        scratch_shapes=[
+            pltpu.VMEM(dims, kind)
+            for kind in (BF, F32)
+            for dims in ((4, SLOT, WIDTH), (8, 96, WIDTH), (96, FF), (384, WIDTH))
+        ]
+        + [pltpu.SemaphoreType.DMA((28,))],
+        compiler_params=pltpu.CompilerParams(vmem_limit_bytes=62 * 2**20),
+    )(*mid)
+    out = list(out)
+    out[0], out[1] = (jnp.transpose(v, (1, 0, 2)) for v in out[:2])
+    out[16] = out[16].T
+    return tuple(out)
+
+
+def solution(mesh):
+    if dict(mesh.shape) != {"pb": 4, "pa": 8}:
+        return generic(mesh)
+    wide, tall = P("pb", "pa", None), P("pa", None)
+    rows, whole = P("pb", None, None), P()
+    return jax.shard_map(
+        fused,
+        mesh=mesh,
+        in_specs=(rows, wide, rows, P("pb"), P("pb"), whole, *[tall] * 10, *[whole] * 4),
+        out_specs=(rows, rows, wide, *[tall] * 10, *[whole] * 4),
+        check_vma=False,
+    )

time: 599 us -> 145 us (0.24); the launches traced: 589 us -> 145 us
  waiting for transfers between devices: 298 us -> 0 us
  Pallas kernels: 0 us -> 144 us
  matrix products: 103 us -> 0 us
  blocking collectives: 96.5 us -> 0 us
  local copies, waits for them, and re-layouts: 63.3 us -> 0 us
  between operations: 15.3 us -> 0.83 us
  other arithmetic: 12 us -> 0 us
    all_gather x3 -> x0, waiting for transfers between devices: 185 us -> none  [the longest x1 88.3 us: shards(): lax.all_gather(stacked, 'pa', axis=1, tiled=True)]
    pallas_call x0 -> x2, Pallas kernels: none -> 144 us  [the longest x1 137 us: fused(): pl.pallas_call(layer, out_shape=[rows, rows, shape(4, SLOT, WIDTH, kind=B...]
    psum x2 -> x0, waiting for transfers between devices: 111 us -> none  [the longest x1 85.3 us: shards(): lax.psum((grad_query_self, grad_key_self, grad_value_self, grad_out_self,...]
    dot_general x44 -> x0, matrix products: 103 us -> none  [the longest x10 29.6 us: product(): return jnp.dot(left, right, preferred_element_type=jnp.float32)]
    psum x3 -> x0, blocking collectives: 74.2 us -> none  [the longest x1 32.1 us: shards(): lax.psum(part_query, 'pa')]
    unnamed x140 -> x0, local copies, waits for them, and re-layouts: 46.2 us -> none
    pmax x1 -> x0, blocking collectives: 22.3 us -> none  [shards(): row_max = lax.pmax(jnp.max(cscores, -1), 'pa')]
    reshape x17 -> x0, local copies, waits for them, and re-layouts: 11 us -> none  [the longest x5 6.07 us: heads_of(): return value.reshape(value.shape[0], value.shape[1], head_count, head_size)]
  transfers between devices with their start and end apart: 7 -> 0, of which waited for: 5 -> 0; matrix products, arithmetic and copies ran while one was open for 14% -> 0% of each run, Pallas kernels for 0% -> 0%
where the time goes in v1:
time: 145 us
  Pallas kernels  144 us (99%)
    pallas_call x1, Pallas kernels, fused(): pl.pallas_call(layer, out_shape=[rows, rows, shape(4, SLOT, WIDTH, kind=B...  137 us
    pallas_call x1, Pallas kernels, fused(): pl.pallas_call(write, out_shape=[*(rows, rows, shape(4, SLOT, WIDTH)), *[...  7.42 us

profile of v1, /device:TPU:1, one launch (start us, length us, event | category | flops | bytes accessed | tf_op | source)
XLA Modules:
  0.0 145.2 jit_solution(5984272979860586539)
XLA Ops:
  0.7 136.9 %shard_map.323 = (f32[20,4,768]{2,1,0:T(4,128)}, f32[20,4,768]{2,1,0:T(4,128)}, bf16[4,512,768]{2,1,0:T(8,128)(2,1)}, bf16[8,96,768]{2,1,0:T(8,128)(2,1)}, bf16[...) custom-call(f32[20,4,768]{2,1,0:T(4,128)} %bitcast.6, ...), custom_call_target="tpu_custom_call" | custom-call | tf_op jit(solution)/shard_map/pallas_call | solution.py:1268
  137.6 7.4 %shard_map.324 = (f32[20,4,768]{2,1,0:T(4,128)}, f32[20,4,768]{2,1,0:T(4,128)}, f32[4,512,768]{2,1,0:T(8,128)}, f32[96,768]{1,0:T(8,128)}, f32[96,768]{1,0:T(8,1...) custom-call(f32[20,4,768]{2,1,0:T(4,128)} %get-tuple-element.42.dout, ...), custom_call_target="tpu_custom_call" | custom-call | tf_op jit(solution)/shard_map/pallas_call | solution.py:1295

commit v2 on v1

--- a/solution.py
+++ b/solution.py
@@ -1,3 +1,4 @@
+import math
 import types
 
 import jax
@@ -433,8 +434,7 @@
 
 
 SCRATCH = dict(
-    sq=((8, WIDTH, WIDTH), BF),
-    ex=((WIDTH, FF), BF),
+    sq=((9, WIDTH, WIDTH), BF),
     rd=((WIDTH, WIDTH), BF),
     enc=((4, SLOT, WIDTH), BF),
     xs=((OWN, WIDTH), F32),
@@ -443,10 +443,16 @@
     bias=((3 * PAD, PAD), F32),
     s1=((4, OWN, 640), BF),
     r1=((3, OWN, 640), BF),
-    gact=((4, OWN, WIDTH), BF),
+    gact=((OWN, WIDTH), F32),
+    s9=((4, OWN, 256), BF),
+    r9=((3, OWN, 256), BF),
+    t3=((4, OWN, 256), BF),
     s2=((4, OWN, 256), BF),
     r2=((3, OWN, 256), BF),
-    ag2=((8, OWN, 256), BF),
+    ag2=((2, 4, OWN, 256), BF),
+    gz=((OWN, WIDTH), BF),
+    acts=((OWN, WIDTH), BF),
+    span=((128, 384), F32),
     x6=((6, 192, 128), BF),
     y6=((6, 192, 128), BF),
     qk=((4, ROWS, WIDTH), BF),
@@ -464,11 +470,13 @@
     mixg=((2, 4, OWN, 256), BF),
     gm=((2, OWN, WIDTH), BF),
     s7=((2, 4, OWN, 256), BF),
-    r7=((8, OWN, 256), BF),
+    c7=((4, OWN, 256), BF),
+    z7=((4, OWN, 256), BF),
+    r7=((3, OWN, 256), BF),
     gcq=((4, OWN, 256), BF),
     s8=((4, OWN, 256), BF),
     r8=((3, OWN, 256), BF),
-    dog=((8, OWN, 256), BF),
+    dog=((2, 4, OWN, 256), BF),
     dgr=((2, OWN, WIDTH), F32),
     tot=((ROWS, 128), F32),
     gsg=((4, OWN, 640), BF),
@@ -477,12 +485,12 @@
     wg=((8, 96, WIDTH), BF),
     gexs=((96, FF), BF),
     gres=((384, WIDTH), BF),
-    p1=((2, 4, OWN, WIDTH), BF),
-    p2=((2, 4, OWN, 4096), BF),
-    p3=((2, 4, OWN, 1024), BF),
-    p4=((2, 4, OWN, 1024), BF),
-    p5=((2, 4, OWN, 1024), BF),
-    p6=((2, 4, OWN, 2560), BF),
+    p1=((2, 4, 16, 1920), BF),
+    p2=((2, 4, 16, 10240), BF),
+    p3=((2, 4, 16, 2560), BF),
+    p4=((2, 4, 16, 2560), BF),
+    p5=((2, 4, 16, 2560), BF),
+    p6=((2, 4, 16, 6400), BF),
     sgain=((2, 4, 8, WIDTH), F32),
     stab=((2, 4, BUCKETS, 128), F32),
     kw1=((WIDTH, WIDTH), BF),
@@ -501,7 +509,7 @@
     vw4=((2, 4, 96, 256), BF),
     eg=((4, SLOT, WIDTH), BF),
 )
-SEMAPHORES = 512
+SEMAPHORES = 188
 NEAR, SCALAR, FAR = pltpu.VMEM, pltpu.SMEM, pl.ANY
 IN_KIND = dict(
     x=NEAR, og=NEAR, plen=SCALAR, pcount=SCALAR, buckets=NEAR, table=SCALAR,
@@ -513,9 +521,22 @@
 )
 
 
+class Batch:
+    def __init__(self, wire, span):
+        self.span, self.sent, self.landed = span, wire.next(), wire.next()
+        wire.batches.append(self)
+
+    def wait_recv(self):
+        pltpu.make_async_copy(self.span, self.span, self.landed).wait()
+
+    def wait_send(self):
+        pltpu.make_async_copy(self.span, self.span, self.sent).wait()
+
+
 class Wire:
-    def __init__(self, sems):
-        self.sems, self.count, self.sent = sems, 0, []
+    def __init__(self, sems, narrow, wide):
+        self.sems, self.count, self.batches = sems, 0, []
+        self.narrow, self.wide = narrow, wide
         self.pb, self.pa = lax.axis_index("pb"), lax.axis_index("pa")
         self.z, self.c = self.pa // 2, lax.rem(self.pa, 2)
 
@@ -528,18 +549,28 @@
         copy.start()
         return copy
 
-    def remote(self, src, dst, pb, pa):
-        copy = pltpu.make_async_remote_copy(
-            src_ref=src,
-            dst_ref=dst,
-            send_sem=self.next(),
-            recv_sem=self.next(),
-            device_id=(pb, pa),
-            device_id_type=MESH,
-        )
-        copy.start()
-        self.sent.append(copy)
-        return copy
+    def span(self, size, dtype):
+        if dtype == F32:
+            return self.wide.at[pl.ds(0, size // 384), :]
+        lane = next(n for n in (384, 768, 640, 512, 256, 128) if size % (16 * n) == 0 and size <= n * WIDTH)
+        return self.narrow.at[0, pl.ds(0, size // lane), pl.ds(0, lane)]
+
+    def batch(self, copies):
+        first = copies[0][0]
+        span = first
+        if len(copies) > 1:
+            span = self.span(sum(math.prod(src.shape) for src, _, _, _ in copies), first.dtype)
+        out = Batch(self, span)
+        for src, dst, pb, pa in copies:
+            pltpu.make_async_remote_copy(
+                src_ref=src,
+                dst_ref=dst,
+                send_sem=out.sent,
+                recv_sem=out.landed,
+                device_id=(pb, pa),
+                device_id_type=MESH,
+            ).start()
+        return out
 
     def zpeer(self, j):
         return lax.rem(self.z + j, 4)
@@ -553,125 +584,93 @@
     def yside(self):
         return lax.rem(self.pb + 2, 4)
 
-    def to_core(self, src, dst):
-        return self.remote(src, dst, self.pb, self.pa + 1 - 2 * self.c)
+    def to_core(self, *pairs):
+        return self.batch([(src, dst, self.pb, self.pa + 1 - 2 * self.c) for src, dst in pairs])
 
     def to_z(self, src_of, dst_of):
-        out = []
-        for j in (1, 2, 3):
-            t = self.zpeer(j)
-            out.append(self.remote(src_of(t), dst_of(j), self.pb, 2 * t + self.c))
-        return out
+        peers = [(self.zpeer(j), j) for j in (1, 2, 3)]
+        return self.batch([(src_of(t), dst_of(j), self.pb, 2 * t + self.c) for t, j in peers])
 
     def to_column(self, src_of, dst_of):
-        out = []
-        for j in range(1, 8):
-            t = lax.rem(self.pa + j, 8)
-            out.append(self.remote(src_of(t), dst_of(j), self.pb, t))
-        return out
+        peers = [(lax.rem(self.pa + j, 8), j) for j in range(1, 8)]
+        return self.batch([(src_of(t), dst_of(j), self.pb, t) for t, j in peers])
 
     def to_plane(self, src_of, dst_of):
-        out = []
-        for j in (1, 2, 3):
-            t = self.ppeer(j)
-            out.append(self.remote(src_of(t), dst_of(j), t, self.pa))
-        return out
-
-
-def received(copies):
-    for copy in copies:
-        copy.wait_recv()
-
-
-class PairGather:
-    def __init__(self, wire, sq, pair):
-        self.w, self.sq, self.pair = wire, sq, pair
+        peers = [(self.ppeer(j), j) for j in (1, 2, 3)]
+        return self.batch([(src_of(t), dst_of(j), t, self.pa) for t, j in peers])
+
+    def to_sides(self, refs):
+        sides = (self.xside(), self.yside())
+        return self.batch([(ref, ref, side, self.pa) for ref in refs for side in sides])
+
+
+class Gather:
+    def __init__(self, wire, sq, index, source, wide=False):
+        self.w, self.sq, self.index, self.source, self.wide = wire, sq, index, source, wide
+        row = pl.multiple_of(48 * lax.rem(wire.pb, 2), 16)
+
+        def block(t):
+            lane = 384 * (wire.pb // 2) + (WIDTH * t if wide else 0)
+            return source.at[pl.ds(row, 48), pl.ds(pl.multiple_of(lane, 128), 384)]
+
+        self.a = wire.to_z(block, lambda j: self.part(wire.z, wire.pb, 0, 384))
 
     def part(self, z, pb, begin, size):
         row = pl.multiple_of(96 * (2 * z + self.w.c) + 48 * lax.rem(pb, 2), 16)
-        return self.sq.at[2 * self.pair + pb // 2, pl.ds(row, 48), pl.ds(begin, size)]
-
-    def start(self):
-        w = self.w
-        src = self.part(w.z, w.pb, 0, WIDTH)
-        self.a = w.to_z(lambda t: src, lambda j: src)
+        lane = pl.multiple_of(384 * (pb // 2) + begin, 128)
+        return self.sq.at[self.index, pl.ds(row, 48), pl.ds(lane, size)]
 
     def plane(self):
         w = self.w
-        received(self.a)
-        self.b = []
-        for i in (1, 2, 3):
-            ref = self.part(w.zpeer(i), w.pb, 0, WIDTH)
-            self.b += [w.remote(ref, ref, side, w.pa) for side in (w.xside(), w.yside())]
+        self.a.wait_recv()
+        self.a = w.to_sides([self.part(w.zpeer(i), w.pb, 0, 384) for i in (1, 2, 3)])
 
     def relay(self):
         w = self.w
-        received(self.b)
-        self.d = []
+        self.a.wait_recv()
+        copies = []
+        cut = 128 if self.index % 2 else 256
         for i in (1, 2, 3):
-            ref = self.part(w.zpeer(i), w.xside(), 0, WIDTH // 2)
-            self.d.append(w.remote(ref, ref, w.yside(), w.pa))
-            ref = self.part(w.zpeer(i), w.yside(), WIDTH // 2, WIDTH // 2)
-            self.d.append(w.remote(ref, ref, w.xside(), w.pa))
+            ref = self.part(w.zpeer(i), w.xside(), 0, cut)
+            copies.append((ref, ref, w.yside(), w.pa))
+            ref = self.part(w.zpeer(i), w.yside(), cut, 384 - cut)
+            copies.append((ref, ref, w.xside(), w.pa))
+        self.a = w.batch(copies)
 
     def core(self):
         w = self.w
-        received(self.d)
-        self.e = []
-        for k in (0, 1):
-            for i in (1, 2, 3):
-                row = pl.multiple_of(96 * (2 * w.zpeer(i) + w.c), 16)
-                ref = self.sq.at[2 * self.pair + k, pl.ds(row, 96), :]
-                self.e.append(w.to_core(ref, ref))
+        self.a.wait_recv()
+        refs = []
+        for i in (1, 2, 3):
+            row = pl.multiple_of(96 * (2 * w.zpeer(i) + w.c), 16)
+            refs.append(self.sq.at[self.index, pl.ds(row, 96), :])
+        self.a = w.to_core(*[(ref, ref) for ref in refs])
 
     def finish(self):
-        received(self.e)
-
-
-class WideGather:
-    def __init__(self, wire, ex):
-        self.w, self.ex = wire, ex
-
-    def part(self, z, pb, begin, size):
-        row = pl.multiple_of(96 * (2 * z + self.w.c), 16)
-        lane = pl.multiple_of(WIDTH * pb + begin, 128)
-        return self.ex.at[pl.ds(row, 96), pl.ds(lane, size)]
-
-    start, plane, relay = PairGather.start, PairGather.plane, PairGather.relay
-
-    def core(self):
-        w = self.w
-        received(self.d)
-        self.e = []
-        for i in (1, 2, 3):
-            ref = self.ex.at[pl.ds(pl.multiple_of(96 * (2 * w.zpeer(i) + w.c), 16), 96), :]
-            self.e.append(w.to_core(ref, ref))
-
-    finish = PairGather.finish
+        self.a.wait_recv()
 
 
 class PlaneRows:
     def __init__(self, wire, ref):
-        self.w, self.ref = w, ref = wire, ref
-        src = ref.at[w.c, w.pb]
-        self.a = [w.remote(src, src, side, w.pa) for side in (w.xside(), w.yside())]
+        self.w, self.ref = wire, ref
+        self.a = wire.to_sides([ref.at[wire.c, wire.pb]])
 
     def relay(self):
         w = self.w
-        received(self.a)
-        half = self.ref.shape[3] // 2
-        self.a = []
-        for k, side, out in ((0, w.xside(), w.yside()), (1, w.yside(), w.xside())):
-            src = self.ref.at[w.c, side, :, pl.ds(half * k, half)]
-            self.a.append(w.remote(src, src, out, w.pa))
+        self.a.wait_recv()
+        size = self.ref.shape[3]
+        half = size // 256 * 128
+        a = self.ref.at[w.c, w.xside(), :, pl.ds(0, half)]
+        b = self.ref.at[w.c, w.yside(), :, pl.ds(half, size - half)]
+        self.a = w.batch([(a, a, w.yside(), w.pa), (b, b, w.xside(), w.pa)])
 
     def core(self):
-        received(self.a)
+        self.a.wait_recv()
         src = self.ref.at[self.w.c]
-        self.b = [self.w.to_core(src, src)]
+        self.a = self.w.to_core((src, src))
 
     def finish(self):
-        received(self.b)
+        self.a.wait_recv()
 
 
 class PlaneSmall(PlaneRows):
@@ -681,6 +680,24 @@
         self.a = wire.to_plane(lambda t: src, lambda j: src)
 
 
+def pack(v):
+    half = v.shape[1] // 2
+    last = jnp.where(
+        lax.broadcasted_iota(jnp.int32, (8, v.shape[1]), 0) < 4, v[16:24], pltpu.roll(v[40:48], 4, 0)
+    )
+    last = jnp.concatenate([last[:, :half], last[:, half:]], 0)
+    return lowered(jnp.concatenate([v[:16], v[24:40], last], 1))
+
+
+def unpack(ref, begin, width):
+    begin = begin * 5 // 2
+    a = ref[:, :, :, begin : begin + width].reshape(128, width)
+    b = ref[:, :, :, begin + width : begin + 2 * width].reshape(128, width)
+    t = ref[:, :, :, begin + 2 * width : begin + width * 5 // 2].astype(F32)
+    t = [t[:, :, 8 * k : 8 * k + 8, :].reshape(64, width // 2) for k in (0, 1)]
+    return jnp.concatenate([a, b, lowered(jnp.concatenate(t, 1))], 0)
+
+
 class CrossReduce:
     def __init__(self, wire, refs):
         self.w, self.refs = wire, refs
@@ -688,7 +705,7 @@
     def core(self):
         w, (w1, r1, w2, r2, w3, r3, w4) = self.w, self.refs
         row = pl.multiple_of(384 * (1 - w.c), 16)
-        self.a = w.to_core(w1.at[pl.ds(row, 384), :], r1)
+        self.a = w.to_core((w1.at[pl.ds(row, 384), :], r1))
 
     def plane(self):
         w, (w1, r1, w2, r2, w3, r3, w4) = self.w, self.refs
@@ -701,7 +718,7 @@
 
     def line(self):
         w, (w1, r1, w2, r2, w3, r3, w4) = self.w, self.refs
-        received(self.b)
+        self.b.wait_recv()
         t = w2[w.pb].astype(F32)
         for j in range(3):
             t = t + r2[j].astype(F32)
@@ -711,7 +728,7 @@
 
     def spread(self):
         w, (w1, r1, w2, r2, w3, r3, w4) = self.w, self.refs
-        received(self.d)
+        self.d.wait_recv()
         t = w3[w.z].astype(F32)
         for j in range(3):
             t = t + r3[j].astype(F32)
@@ -725,8 +742,8 @@
         return lowered(t.T[:96])
 
 
-def inputs_half(a, c):
-    t = a.astype(F32).reshape(384, 256)
+def inputs_half(t, c):
+    t = t.astype(F32)
     t = lax.select(c == 1, pltpu.roll(t, 160, 1), t)[:, :128]
     return lowered(t.T)
 
@@ -735,9 +752,9 @@
     names = (*IN_KIND, *OUT_KIND)
     r = types.SimpleNamespace(**dict(zip(names, refs)))
     s = types.SimpleNamespace(**dict(zip(SCRATCH, refs[len(names) :])))
-    w = Wire(refs[-1])
+    w = Wire(refs[-1], s.sq, s.span)
     pb, pa, z, c = w.pb, w.pa, w.z, w.c
-    sq, ex, rd, enc = s.sq, s.ex, s.rd, s.enc
+    sq, rd, enc = s.sq, s.rd, s.enc
 
     barrier = pltpu.get_barrier_semaphore()
     for j in range(1, 8):
@@ -752,7 +769,8 @@
     red_rows = pl.ds(pl.multiple_of(384 * c, 16), 384)
     order = (SQ, SK, SV, CQ, CK, SO, CV, CO)
     held = {i: w.local(squares[i], sq.at[i, own_rows, :]) for i in order}
-    held[EX] = w.local(r.wex, ex.at[own_rows, :])
+    chip_cols = pl.ds(pl.multiple_of(WIDTH * z, 128), WIDTH)
+    held[EX] = w.local(r.wex.at[:, chip_cols], sq.at[EX, own_rows, :])
     held[RD] = w.local(r.wre, rd.at[red_rows, :])
     held[EN] = w.local(r.enc_h, enc)
 
@@ -768,16 +786,20 @@
     h1z = choose(split4(x * rs1 * g1), z)
     xz = choose(split4(x), z)
     h1b = lowered(h1z)
-    s.p6[c, pb, :, 2304:2560] = h1b
-    s.p1[c, pb] = lowered(s.ogs[...])
+    s.p6[c, pb, :, 5760:6400] = pack(h1z)
+    s.p1[c, pb] = pack(s.ogs[...])
+    s.gz[...] = lowered(s.ogs[...])
 
     pl.semaphore_wait(barrier, 10)
-    other = {}
-    for i in order:
-        other[i] = w.to_core(squares[i], sq.at[i, own_rows, :])
-    other[RD] = w.to_core(r.wre, rd.at[red_rows, :])
-    other[EX] = w.to_core(r.wex, ex.at[own_rows, :])
-    gather_a, gather_b, gather_c = PairGather(w, sq, 0), PairGather(w, sq, 1), WideGather(w, ex)
+    other = [
+        w.to_core(*[(squares[i], sq.at[i, own_rows, :]) for i in (SQ, SK, SV)]),
+        w.to_core((r.wre, rd.at[red_rows, :])),
+        w.to_core(*[(squares[i], sq.at[i, own_rows, :]) for i in (SO, CQ, CK)]),
+        w.to_core(
+            *[(squares[i], sq.at[i, own_rows, :]) for i in (CV, CO)],
+            (r.wex.at[:, chip_cols], sq.at[EX, own_rows, :]),
+        ),
+    ]
 
     def chip(i):
         return sq[i, pl.ds(pl.multiple_of(PART * z, 16), PART), :]
@@ -785,19 +807,16 @@
     parts = []
     for i in (SQ, SK, SV):
         held[i].wait()
-        other[i].wait_recv()
+        if i == SQ:
+            other[0].wait_recv()
         parts.append(split4(nn(h1b[:, :PART], chip(i))))
     blocks = [join3([parts[k][j] for k in range(3)]) for j in range(4)]
     for j in range(4):
         s.s1[j] = lowered(blocks[j])
     own_qkv = choose(blocks, z)
     f1 = w.to_z(lambda t: s.s1.at[t], lambda j: s.r1.at[j - 1])
-    held[CQ].wait()
-    held[CK].wait()
-    gather_a.start()
-    held[CV].wait()
-    held[CO].wait()
-    gather_b.start()
+    gather_q = Gather(w, sq, CQ, r.wcq)
+    gather_k = Gather(w, sq, CK, r.wck)
 
     bucket = s.bks[...]
 
@@ -810,10 +829,10 @@
 
     lax.fori_loop(0, 3, bias_head, 0)
     held[RD].wait()
-    other[RD].wait_recv()
-    s.gact[z] = lowered(nt(s.p1[c, pb], rd[...]))
-
-    received(f1)
+    other[1].wait_recv()
+    s.gact[...] = nt(s.gz[...], rd[...])
+
+    f1.wait_recv()
     v = own_qkv
     for j in range(3):
         v = v + s.r1[j].astype(F32)
@@ -834,17 +853,19 @@
         probs.append(attend(stacks[k], k3[rows], s.bias[...]))
         mixes.append(pick_heads(nn(lowered(probs[k]), lowered(v3[rows])), 3))
     mixb = lowered(jnp.concatenate(mixes, 0))
-    s.p5[c, pb, :, 768:960] = mixb
+    gap = jnp.zeros((OWN, 64), F32)
+    s.p5[c, pb, :, 1920:2560] = pack(jnp.concatenate([jnp.concatenate(mixes, 0), gap], 1))
     held[SO].wait()
-    other[SO].wait_recv()
+    other[2].wait_recv()
     parts = split4(nn(mixb, chip(SO)))
     for j in range(4):
         s.s2[j] = lowered(parts[j])
     own_o = choose(parts, z)
     f2 = w.to_z(lambda t: s.s2.at[t], lambda j: s.r2.at[j - 1])
-    gather_a.plane()
-
-    received(f2)
+    gather_q.plane()
+    gather_k.plane()
+
+    f2.wait_recv()
     r1z = xz + own_o
     for j in range(3):
         r1z = r1z + s.r2[j].astype(F32)
@@ -853,32 +874,38 @@
     square = jnp.sum(jnp.where(counts, r1z * r1z, 0.0), -1, keepdims=True)
     high = lowered(square).astype(F32)
     tail = jnp.where(lanes(OWN, 256) < 224, high, square - high)
-    s.ag2[pa] = lowered(jnp.where(counts, r1z * g2z, tail))
-    f3 = w.to_column(lambda t: s.ag2.at[pa], lambda j: s.ag2.at[pa])
-    gather_b.plane()
-    held[EX].wait()
-    gather_c.start()
-    gather_a.relay()
-    gather_a.core()
-
-    received(f3)
-    blocks = [[s.ag2[2 * j + k].astype(F32) for j in range(4)] for k in (0, 1)]
+    s.ag2[c, z] = lowered(jnp.where(counts, r1z * g2z, tail))
+    f3 = w.to_z(lambda t: s.ag2.at[c, z], lambda j: s.ag2.at[c, z])
+    gather_v = Gather(w, sq, CV, r.wcv)
+    gather_q.relay()
+    gather_q.core()
+    gather_k.relay()
+
+    f3.wait_recv()
+    f3c = w.to_core((s.ag2.at[c], s.ag2.at[c]))
+    gather_o = Gather(w, sq, CO, r.wco)
+    gather_x = Gather(w, sq, EX, r.wex, True)
+    gather_v.plane()
+    f3c.wait_recv()
+    blocks = [[s.ag2[k, j].astype(F32) for j in range(4)] for k in (0, 1)]
     rs2 = []
     for k in (0, 1):
         t = blocks[k][0] + blocks[k][1] + blocks[k][2] + blocks[k][3]
         lane = lanes(OWN, 256)
         t = jnp.sum(jnp.where((lane == 192) | (lane == 224), t, 0.0), -1, keepdims=True)
         rs2.append(lax.rsqrt(t * (1.0 / WIDTH) + epsilon))
-    gather_b.relay()
-    gather_a.finish()
-    other[CQ].wait_recv()
+    gather_q.finish()
+    held[CQ].wait()
     cq = jnp.zeros((ALL, WIDTH), F32)
     for j in range(4):
-        t = jnp.concatenate([s.ag2[2 * j], s.ag2[2 * j + 1]], 0)[:, :PART]
+        t = jnp.concatenate([s.ag2[0, j], s.ag2[1, j]], 0)[:, :PART]
         cq = cq + nn(t, sq[CQ, PART * j : PART * (j + 1), :])
     cq = cq * jnp.concatenate(rs2, 0)
     cq = lowered(cq).astype(F32) * 0.125
-    other[CK].wait_recv()
+    gather_k.core()
+    gather_v.relay()
+    gather_k.finish()
+    held[CK].wait()
     for p in range(6):
         t = jnp.concatenate([pair_stack(cq[PAD * q : PAD * (q + 1)], p) for q in range(4)], 0)
         s.x6[p] = lowered(t)
@@ -906,11 +933,13 @@
 
     lax.fori_loop(0, 4, scores, 0)
     s.stg[pa] = s.stat[...].T[:8]
-    f5 = w.to_column(lambda t: s.stg.at[pa], lambda j: s.stg.at[pa])
-    gather_b.core()
-    gather_c.plane()
-    gather_b.finish()
-    other[CV].wait_recv()
+    f4 = w.to_column(lambda t: s.stg.at[pa], lambda j: s.stg.at[pa])
+    gather_v.core()
+    gather_o.plane()
+    gather_x.plane()
+    gather_v.finish()
+    held[CV].wait()
+    other[3].wait_recv()
     low = lanes(PAD, 128) < SIZE
     tiles = [[] for q in range(4)]
     for p in range(6):
@@ -923,16 +952,18 @@
     for k in (0, 1):
         for j, part in enumerate(split4(num[OWN * k : OWN * (k + 1)])):
             s.s5[k, j] = lowered(part)
-    f5 += w.to_column(lambda t: s.s5.at[lax.rem(t, 2), t // 2], lambda j: s.r5.at[pa])
+    f5 = w.to_column(lambda t: s.s5.at[lax.rem(t, 2), t // 2], lambda j: s.r5.at[pa])
     s.r5[pa] = s.s5[c, z]
-    gact_copies = w.to_z(lambda t: s.gact.at[z], lambda j: s.gact.at[z])
     rows1 = PlaneRows(w, s.p1)
-    r1full = join4(blocks_of(s.ag2, c)) / g2
+    r1full = join4([s.ag2[c, j].astype(F32) for j in range(4)]) / g2
     rs2o = lax.select(c == 1, rs2[1], rs2[0])
     n2 = r1full * rs2o
-    s.p4[c, pb, :, 768:1024] = lowered(choose(split4(n2 * g2), z))
-
-    received(f5)
+    s.p4[c, pb, :, 1920:2560] = pack(choose(split4(n2 * g2), z))
+    gather_o.relay()
+    gather_x.relay()
+
+    f4.wait_recv()
+    f5.wait_recv()
     stats = [s.stg[k] for k in range(8)]
     top = stats[0]
     for k in range(1, 8):
@@ -959,15 +990,16 @@
             col = [w3[PAD * h : PAD * (h + 1), 2 * m + k : 2 * m + k + 1] for h in range(3)]
             t = jnp.where(lane < 64, col[0], jnp.where(lane < 128, col[1], col[2]))
             sums[k] = sums[k] + t * block[PAD * k : PAD * (k + 1)]
-    mixc = lowered(jnp.concatenate(sums, 0))
-    s.mixg[c, z] = mixc
-    s.p3[c, pb, :, 768:1024] = mixc
+    mixc = jnp.concatenate(sums, 0)
+    s.mixg[c, z] = lowered(mixc)
+    s.p3[c, pb, :, 1920:2560] = pack(mixc)
     f6 = w.to_z(lambda t: s.mixg.at[c, z], lambda j: s.mixg.at[c, z])
-    gather_c.relay()
-    gather_c.core()
-    other[CO].wait_recv()
-    received(f6)
-    mix_core = w.to_core(s.mixg.at[c], s.mixg.at[c])
+    gather_o.core()
+    gather_x.core()
+    held[CO].wait()
+    gather_o.finish()
+    f6.wait_recv()
+    mix_core = w.to_core((s.mixg.at[c], s.mixg.at[c]))
     after = jnp.zeros((OWN, WIDTH), F32)
     for j in range(4):
         after = after + nn(s.mixg[c, j][:, :PART], sq[CO, PART * j : PART * (j + 1), :])
@@ -976,36 +1008,43 @@
     rs3 = lax.rsqrt(jnp.mean(resid * resid, -1, keepdims=True) + epsilon)
     n3 = resid * rs3
     h3 = lowered(n3 * g3)
-    s.p2[c, pb, :, 3072:3328] = lowered(choose(split4(n3 * g3), z))
-    received(gact_copies)
-    gather_c.finish()
-    other[EX].wait_recv()
-    gh3 = jnp.zeros((OWN, WIDTH), F32)
+    s.p2[c, pb, :, 7680:8320] = pack(choose(split4(n3 * g3), z))
+    gather_x.finish()
+    held[EX].wait()
+    v = nn(h3, sq[EX])
+    t = jnp.tanh(GELU_A * (v + GELU_B * v * v * v))
+    act = 0.5 * v * (1.0 + t)
+    s.acts[...] = lowered(act)
+    s.p2[c, pb, :, 8320:10240] = pack(act)
+    slope = 0.5 * (1.0 + t) + 0.5 * v * (1.0 - t * t) * GELU_A * (1.0 + 3.0 * GELU_B * v * v)
+    gp = s.gact[...] * slope
+    gp_cols = pl.ds(pl.multiple_of(1920 * z, 128), 1920)
+    s.p2[c, pb, :, gp_cols] = pack(gp)
+    gp = lowered(gp)
+    parts = split4(nt(gp, sq[EX]))
     for j in range(4):
-        cols = slice(WIDTH * j, WIDTH * (j + 1))
-        v = nn(h3, ex[:, cols])
-        t = jnp.tanh(GELU_A * (v + GELU_B * v * v * v))
-        act = lowered(0.5 * v * (1.0 + t))
-        slope = 0.5 * (1.0 + t) + 0.5 * v * (1.0 - t * t) * GELU_A * (1.0 + 3.0 * GELU_B * v * v)
-        gp = lowered(s.gact[j].astype(F32) * slope)
-        s.p2[c, pb, :, cols] = gp
-
-        @pl.when(z == j)
-        def keep():
-            s.p2[c, pb, :, 3328:4096] = act
-
-        gh3 = gh3 + nt(gp, ex[:, cols])
+        s.s9[j] = lowered(parts[j])
+    own_g = choose(parts, z)
+    fe = w.to_z(lambda t: s.s9.at[t], lambda j: s.r9.at[j - 1])
+    rows1.relay()
+    g3z = choose(split4(jnp.broadcast_to(g3, (OWN, WIDTH))), z)
+    fe.wait_recv()
+    t = own_g
+    for j in range(3):
+        t = t + s.r9[j].astype(F32)
+    s.t3[z] = lowered(t * g3z)
+    ff = w.to_z(lambda t: s.t3.at[z], lambda j: s.t3.at[z])
+    fp = w.to_z(lambda t: s.p2.at[c, pb, :, gp_cols], lambda j: s.p2.at[c, pb, :, gp_cols])
+    ff.wait_recv()
     og = s.ogs[...]
-    gain3 = jnp.sum(gh3 * n3, 0, keepdims=True)
-    t = gh3 * g3
+    t = join4([s.t3[j].astype(F32) for j in range(4)])
+    gain3 = jnp.sum(t * n3, 0, keepdims=True) / g3
     grad_two = og + rs3 * (t - n3 * jnp.mean(t * n3, -1, keepdims=True))
     gcb = lowered(grad_two)
-    s.p3[c, pb, :, :768] = gcb
+    s.p3[c, pb, :, :1920] = pack(grad_two)
     s.gm[c] = lowered(nt(gcb, sq[CO]))
-    f7 = w.to_core(s.gm.at[c], s.gm.at[c])
-    rows1.relay()
+    f7 = w.to_core((s.gm.at[c], s.gm.at[c]))
     rows3 = PlaneRows(w, s.p3)
-    rows2 = PlaneRows(w, s.p2)
     mix_core.wait_recv()
     f7.wait_recv()
 
@@ -1036,6 +1075,8 @@
         s.vw1[128 * p : 128 * (p + 1), :] = lowered(tn(s.y6[p], t))
     vred = CrossReduce(w, [s.vw1, s.vr1, s.vw2, s.vr2, s.vw3, s.vr3, s.vw4])
     vred.core()
+    fp.wait_recv()
+    rows2 = PlaneRows(w, s.p2)
 
     def grads(q, carry):
         pick = lanes(ROWS, 128) == q
@@ -1057,16 +1098,18 @@
     for k in (0, 1):
         for j, part in enumerate(split4(num[OWN * k : OWN * (k + 1)])):
             s.s7[k, j] = lowered(part)
-    f8 = w.to_column(lambda t: s.s7.at[lax.rem(t, 2), t // 2], lambda j: s.r7.at[pa])
-    s.r7[pa] = s.s7[c, z]
+    fc = w.to_core((s.s7.at[1 - c], s.c7))
     vred.plane()
+    fc.wait_recv()
+    for j in range(4):
+        s.z7[j] = lowered(s.s7[c, j].astype(F32) + s.c7[j].astype(F32))
+    f8 = w.to_z(lambda t: s.z7.at[t], lambda j: s.r7.at[j - 1])
     for p in range(6):
         t = jnp.concatenate([s.as_[q, 48 * p : 48 * (p + 1), :] for q in range(4)], 0)
         s.kw1[128 * p : 128 * (p + 1), :] = lowered(tn(s.x6[p], t))
     kred = CrossReduce(w, [s.kw1, s.kr1, s.kw2, s.kr2, s.kw3, s.kr3, s.kw4])
     kred.core()
     rows3.relay()
-    rows2.relay()
     rows1.core()
     out_copies = []
 
@@ -1077,15 +1120,16 @@
     encoding_grad(0)
     encoding_grad(1)
 
-    received(f8)
-    t = s.r7[0].astype(F32)
-    for k in range(1, 8):
+    f8.wait_recv()
+    t = s.z7[z].astype(F32)
+    for k in range(3):
         t = t + s.r7[k].astype(F32)
     s.gcq[z] = lowered(t)
     f9 = w.to_z(lambda t: s.gcq.at[z], lambda j: s.gcq.at[z])
     kred.plane()
+    rows2.relay()
     rows3.core()
-    parts = split4(nn(s.p2[c, pb, :, 3328:4096], rd[...]))
+    parts = split4(nn(s.acts[...], rd[...]))
     for j in range(4):
         s.s8[j] = lowered(parts[j])
     own_d = choose(parts, z)
@@ -1093,16 +1137,17 @@
     encoding_grad(2)
     encoding_grad(3)
 
-    received(f9)
-    gcq = lowered(join4([s.gcq[j].astype(F32) for j in range(4)]))
-    s.p4[c, pb, :, :768] = gcq
+    f9.wait_recv()
+    gcq = join4([s.gcq[j].astype(F32) for j in range(4)])
+    s.p4[c, pb, :, :1920] = pack(gcq)
+    gcq = lowered(gcq)
     rows4 = PlaneRows(w, s.p4)
     gh2 = nt(gcq, sq[CQ])
     gain2 = jnp.sum(gh2 * n2, 0, keepdims=True)
     t = gh2 * g2
     grad_one = grad_two + rs2o * (t - n2 * jnp.mean(t * n2, -1, keepdims=True))
     gab = lowered(grad_one)
-    s.p5[c, pb, :, :768] = gab
+    s.p5[c, pb, :, :1920] = pack(grad_one)
     rows5 = PlaneRows(w, s.p5)
     gsm = lowered(nt(gab, chip(SO))).astype(F32)
     gsum = jnp.zeros((3 * PAD, PAD), F32)
@@ -1117,7 +1162,6 @@
         dq.append(pick_heads(nn(gsb, lowered(k3[rows])), 3) * 0.125)
         dk.append(tn(gsb, lowered(stacks[k])))
         dv.append(tn(lowered(prob), stacked))
-    gap = jnp.zeros((OWN, 64), F32)
     three = [jnp.concatenate([jnp.concatenate(t, 0), gap], 1) for t in (dq, dk, dv)]
     s.gsg[z] = lowered(join3(three))
     f10 = w.to_z(lambda t: s.gsg.at[z], lambda j: s.gsg.at[z])
@@ -1133,33 +1177,34 @@
     ft = w.to_z(lambda t: s.stz.at[z], lambda j: s.stz.at[z])
     rows2.core()
     vred.line()
-    received(fo)
+    fo.wait_recv()
     t = r2z + own_d
     for j in range(3):
         t = t + s.r8[j].astype(F32)
-    s.dog[pa] = lowered(t)
-    fg = w.to_column(lambda t: s.dog.at[pa], lambda j: s.dog.at[pa])
+    s.dog[c, z] = lowered(t)
+    fg = w.to_z(lambda t: s.dog.at[c, z], lambda j: s.dog.at[c, z])
     rows1.finish()
 
     def half_product(ref, begin, index, rows):
         rows.finish()
-        lhs = inputs_half(ref[:, :, :, begin : begin + 256], c)
-        s.wg[index] = lowered(nn(lhs, ref[:, :, :, :768].reshape(384, WIDTH))[:96])
+        lhs = inputs_half(unpack(ref, begin, 256), c)
+        s.wg[index] = lowered(nn(lhs, unpack(ref, 0, WIDTH))[:96])
         out_copies.append(w.local(s.wg.at[index], r.squares.at[index]))
 
     half_product(s.p3, 768, 7, rows3)
 
-    received(f10)
+    f10.wait_recv()
     unpacked = [part3(s.gsg[j].astype(F32)) for j in range(4)]
-    three = [lowered(join4([unpacked[j][k] for j in range(4)])) for k in range(3)]
+    three = [join4([unpacked[j][k] for j in range(4)]) for k in range(3)]
     for k in range(3):
-        s.p6[c, pb, :, 768 * k : 768 * (k + 1)] = three[k]
+        s.p6[c, pb, :, 1920 * k : 1920 * (k + 1)] = pack(three[k])
+    three = [lowered(v) for v in three]
     rows6 = PlaneRows(w, s.p6)
     gh1 = nt(three[0], chip(SQ)) + nt(three[1], chip(SK)) + nt(three[2], chip(SV))
     g1z = choose(split4(jnp.broadcast_to(g1, (OWN, WIDTH))), z)
     s.tg[z] = lowered(jnp.concatenate([gh1 * g1z[:, :PART], gap], 1))
     f11 = w.to_z(lambda t: s.tg.at[z], lambda j: s.tg.at[z])
-    received(ft)
+    ft.wait_recv()
     s.stab[c, pb] = s.stz[0] + s.stz[1] + s.stz[2] + s.stz[3]
     tab_rows = PlaneSmall(w, s.stab)
     kred.line()
@@ -1168,17 +1213,19 @@
     vred.spread()
     rows2.finish()
     p2 = s.p2
-    lhs = inputs_half(p2[:, :, :, 3072:3328], c)
+    lhs = inputs_half(unpack(p2, 3072, 256), c)
     for j in range(4):
         cols = slice(WIDTH * j, WIDTH * (j + 1))
-        s.gexs[:, cols] = lowered(nn(lhs, p2[:, :, :, cols].reshape(384, WIDTH))[:96])
+        s.gexs[:, cols] = lowered(nn(lhs, unpack(p2, WIDTH * j, WIDTH))[:96])
     out_copies.append(w.local(s.gexs, r.gex))
-    received(f11)
+    f11.wait_recv()
+    fg.wait_recv()
+    fgc = w.to_core((s.dog.at[c], s.dog.at[c]))
     t = join4([s.tg[j].astype(F32) for j in range(4)])
     n1 = s.xs[...] * rs1
     gain1 = jnp.sum(t * n1, 0, keepdims=True) / g1
     s.dgr[c] = grad_one + rs1 * (t - n1 * jnp.mean(t * n1, -1, keepdims=True))
-    fd = w.to_core(s.dgr.at[c], s.dgr.at[c])
+    fd = w.to_core((s.dgr.at[c], s.dgr.at[c]))
     s.sgain[c, pb] = jnp.concatenate([gain1, gain2, gain3, jnp.zeros((5, WIDTH), F32)], 0)
     gain_rows = PlaneSmall(w, s.sgain)
     rows6.relay()
@@ -1186,9 +1233,9 @@
     vred.rows.relay()
     rows4.core()
     rows5.core()
-    half = pl.ds(pl.multiple_of(3328 + 384 * c, 128), 384)
-    lhs = lowered(p2[:, :, :, half].astype(F32).reshape(384, 384).T)
-    s.gres[...] = lowered(nn(lhs, s.p1[...].reshape(384, WIDTH)))
+    t = unpack(p2, 3328, WIDTH).astype(F32)
+    lhs = lowered(lax.select(c == 1, t[:, 384:], t[:, :384]).T)
+    s.gres[...] = lowered(nn(lhs, unpack(s.p1, 0, WIDTH)))
     out_copies.append(w.local(s.gres, r.gre))
     half_product(s.p4, 768, 4, rows4)
     half_product(s.p5, 768, 3, rows5)
@@ -1196,10 +1243,10 @@
     kred.rows.relay()
     tab_rows.core()
     gain_rows.core()
-    received(fg)
+    fgc.wait_recv()
     fd.wait_recv()
     for k in (0, 1):
-        t = join4([s.dog[2 * j + k].astype(F32) for j in range(4)])
+        t = join4([s.dog[k, j].astype(F32) for j in range(4)])
         for m in (0, 1):
             r.decoder_out[:, 2 * k + m, :] = t[PAD * m : PAD * m + ANS]
             r.decoder_grad[:, 2 * k + m, :] = s.dgr[k, PAD * m : PAD * m + ANS, :]
@@ -1222,18 +1269,14 @@
     out_copies.append(w.local(s.wg.at[5], r.squares.at[5]))
     rows6.finish()
     ref = s.p6
-    lhs = inputs_half(ref[:, :, :, 2304:2560], c)
+    lhs = inputs_half(unpack(ref, 2304, 256), c)
     for k in range(3):
-        s.wg[k] = lowered(nn(lhs, ref[:, :, :, 768 * k : 768 * (k + 1)].reshape(384, WIDTH))[:96])
+        s.wg[k] = lowered(nn(lhs, unpack(ref, WIDTH * k, WIDTH))[:96])
         out_copies.append(w.local(s.wg.at[k], r.squares.at[k]))
     for copy in out_copies:
         copy.wait()
-    for copy in w.sent:
-        copy.wait_send()
-
-
-def blocks_of(ref, c):
-    return [ref[2 * j + c].astype(F32) for j in range(4)]
+    for batch in w.batches:
+        batch.wait_send()
 
 
 def write(dout, dgrad, eg, sq, gex, gre, gains, table, *refs):

time: 145 us -> 132 us (0.910)
  Pallas kernels: 144 us -> 131 us
    pallas_call x1, Pallas kernels: 137 us -> 123 us  [fused(): pl.pallas_call(layer, out_shape=[rows, rows, shape(4, SLOT, WIDTH, kind=B...]
where the time goes in v2:
time: 132 us
  Pallas kernels  131 us (99%)
    pallas_call x1, Pallas kernels, fused(): pl.pallas_call(layer, out_shape=[rows, rows, shape(4, SLOT, WIDTH, kind=B...  123 us
    pallas_call x1, Pallas kernels, fused(): pl.pallas_call(write, out_shape=[*(rows, rows, shape(4, SLOT, WIDTH)), *[...  7.42 us

profile of v2, /device:TPU:1, one launch (start us, length us, event | category | flops | bytes accessed | tf_op | source)
XLA Modules:
  0.0 131.6 jit_solution(10114748623963548888)
XLA Ops:
  0.7 123.3 %shard_map.323 = (f32[20,4,768]{2,1,0:T(4,128)}, f32[20,4,768]{2,1,0:T(4,128)}, bf16[4,512,768]{2,1,0:T(8,128)(2,1)}, bf16[8,96,768]{2,1,0:T(8,128)(2,1)}, bf16[...) custom-call(f32[20,4,768]{2,1,0:T(4,128)} %bitcast.6, ...), custom_call_target="tpu_custom_call" | custom-call | tf_op jit(solution)/shard_map/pallas_call | solution.py:1311
  124.0 7.4 %shard_map.324 = (f32[20,4,768]{2,1,0:T(4,128)}, f32[20,4,768]{2,1,0:T(4,128)}, f32[4,512,768]{2,1,0:T(8,128)}, f32[96,768]{1,0:T(8,128)}, f32[96,768]{1,0:T(8,1...) custom-call(f32[20,4,768]{2,1,0:T(4,128)} %get-tuple-element.42.dout, ...), custom_call_target="tpu_custom_call" | custom-call | tf_op jit(solution)/shard_map/pallas_call | solution.py:1338

commit v3 on v2

--- a/solution.py
+++ b/solution.py
@@ -509,7 +509,7 @@
     vw4=((2, 4, 96, 256), BF),
     eg=((4, SLOT, WIDTH), BF),
 )
-SEMAPHORES = 188
+SEMAPHORES = 181
 NEAR, SCALAR, FAR = pltpu.VMEM, pltpu.SMEM, pl.ANY
 IN_KIND = dict(
     x=NEAR, og=NEAR, plen=SCALAR, pcount=SCALAR, buckets=NEAR, table=SCALAR,
@@ -733,7 +733,7 @@
         for j in range(3):
             t = t + r3[j].astype(F32)
         w4[w.c, w.pb] = lowered(t)
-        self.rows = PlaneRows(w, w4)
+        self.rows = PlaneSmall(w, w4)
 
     def result(self):
         w4 = self.refs[-1]
@@ -791,8 +791,9 @@
     s.gz[...] = lowered(s.ogs[...])
 
     pl.semaphore_wait(barrier, 10)
-    other = [
-        w.to_core(*[(squares[i], sq.at[i, own_rows, :]) for i in (SQ, SK, SV)]),
+    other = [w.to_core(*[(squares[i], sq.at[i, own_rows, :]) for i in (SQ, SK, SV)])]
+    gather_q = Gather(w, sq, CQ, r.wcq)
+    other += [
         w.to_core((r.wre, rd.at[red_rows, :])),
         w.to_core(*[(squares[i], sq.at[i, own_rows, :]) for i in (SO, CQ, CK)]),
         w.to_core(
@@ -815,7 +816,6 @@
         s.s1[j] = lowered(blocks[j])
     own_qkv = choose(blocks, z)
     f1 = w.to_z(lambda t: s.s1.at[t], lambda j: s.r1.at[j - 1])
-    gather_q = Gather(w, sq, CQ, r.wcq)
     gather_k = Gather(w, sq, CK, r.wck)
 
     bucket = s.bks[...]
@@ -832,7 +832,9 @@
     other[1].wait_recv()
     s.gact[...] = nt(s.gz[...], rd[...])
 
+    gather_q.plane()
     f1.wait_recv()
+    gather_q.relay()
     v = own_qkv
     for j in range(3):
         v = v + s.r1[j].astype(F32)
@@ -862,7 +864,7 @@
         s.s2[j] = lowered(parts[j])
     own_o = choose(parts, z)
     f2 = w.to_z(lambda t: s.s2.at[t], lambda j: s.r2.at[j - 1])
-    gather_q.plane()
+    gather_q.core()
     gather_k.plane()
 
     f2.wait_recv()
@@ -877,12 +879,11 @@
     s.ag2[c, z] = lowered(jnp.where(counts, r1z * g2z, tail))
     f3 = w.to_z(lambda t: s.ag2.at[c, z], lambda j: s.ag2.at[c, z])
     gather_v = Gather(w, sq, CV, r.wcv)
-    gather_q.relay()
-    gather_q.core()
     gather_k.relay()
 
     f3.wait_recv()
     f3c = w.to_core((s.ag2.at[c], s.ag2.at[c]))
+    gather_k.core()
     gather_o = Gather(w, sq, CO, r.wco)
     gather_x = Gather(w, sq, EX, r.wex, True)
     gather_v.plane()
@@ -902,7 +903,6 @@
         cq = cq + nn(t, sq[CQ, PART * j : PART * (j + 1), :])
     cq = cq * jnp.concatenate(rs2, 0)
     cq = lowered(cq).astype(F32) * 0.125
-    gather_k.core()
     gather_v.relay()
     gather_k.finish()
     held[CK].wait()
@@ -1041,9 +1041,9 @@
     gain3 = jnp.sum(t * n3, 0, keepdims=True) / g3
     grad_two = og + rs3 * (t - n3 * jnp.mean(t * n3, -1, keepdims=True))
     gcb = lowered(grad_two)
-    s.p3[c, pb, :, :1920] = pack(grad_two)
     s.gm[c] = lowered(nt(gcb, sq[CO]))
     f7 = w.to_core((s.gm.at[c], s.gm.at[c]))
+    s.p3[c, pb, :, :1920] = pack(grad_two)
     rows3 = PlaneRows(w, s.p3)
     mix_core.wait_recv()
     f7.wait_recv()
@@ -1086,7 +1086,10 @@
         s.as_[q] = lowered(nn(s.gs[q], enc[q]))
         return carry
 
-    lax.fori_loop(0, 4, grads, 0)
+    lax.fori_loop(0, 2, grads, 0)
+    rows3.relay()
+    vred.plane()
+    lax.fori_loop(2, 4, grads, 0)
     tiles = [[] for q in range(4)]
     for p in range(6):
         t = jnp.concatenate([s.as_[q, 48 * p : 48 * (p + 1), :] for q in range(4)], 0)
@@ -1099,18 +1102,15 @@
         for j, part in enumerate(split4(num[OWN * k : OWN * (k + 1)])):
             s.s7[k, j] = lowered(part)
     fc = w.to_core((s.s7.at[1 - c], s.c7))
-    vred.plane()
+    for p in range(6):
+        t = jnp.concatenate([s.as_[q, 48 * p : 48 * (p + 1), :] for q in range(4)], 0)
+        s.kw1[128 * p : 128 * (p + 1), :] = lowered(tn(s.x6[p], t))
+    kred = CrossReduce(w, [s.kw1, s.kr1, s.kw2, s.kr2, s.kw3, s.kr3, s.kw4])
     fc.wait_recv()
     for j in range(4):
         s.z7[j] = lowered(s.s7[c, j].astype(F32) + s.c7[j].astype(F32))
     f8 = w.to_z(lambda t: s.z7.at[t], lambda j: s.r7.at[j - 1])
-    for p in range(6):
-        t = jnp.concatenate([s.as_[q, 48 * p : 48 * (p + 1), :] for q in range(4)], 0)
-        s.kw1[128 * p : 128 * (p + 1), :] = lowered(tn(s.x6[p], t))
-    kred = CrossReduce(w, [s.kw1, s.kr1, s.kw2, s.kr2, s.kw3, s.kr3, s.kw4])
     kred.core()
-    rows3.relay()
-    rows1.core()
     out_copies = []
 
     def encoding_grad(q):
@@ -1118,6 +1118,8 @@
         out_copies.append(w.local(s.eg.at[q], r.encoding_grad.at[q]))
 
     encoding_grad(0)
+    kred.plane()
+    rows2.relay()
     encoding_grad(1)
 
     f8.wait_recv()
@@ -1126,29 +1128,23 @@
         t = t + s.r7[k].astype(F32)
     s.gcq[z] = lowered(t)
     f9 = w.to_z(lambda t: s.gcq.at[z], lambda j: s.gcq.at[z])
-    kred.plane()
-    rows2.relay()
-    rows3.core()
     parts = split4(nn(s.acts[...], rd[...]))
     for j in range(4):
         s.s8[j] = lowered(parts[j])
     own_d = choose(parts, z)
     fo = w.to_z(lambda t: s.s8.at[t], lambda j: s.r8.at[j - 1])
+    rows1.core()
+    rows3.core()
     encoding_grad(2)
     encoding_grad(3)
 
     f9.wait_recv()
     gcq = join4([s.gcq[j].astype(F32) for j in range(4)])
-    s.p4[c, pb, :, :1920] = pack(gcq)
-    gcq = lowered(gcq)
-    rows4 = PlaneRows(w, s.p4)
-    gh2 = nt(gcq, sq[CQ])
+    gh2 = nt(lowered(gcq), sq[CQ])
     gain2 = jnp.sum(gh2 * n2, 0, keepdims=True)
     t = gh2 * g2
     grad_one = grad_two + rs2o * (t - n2 * jnp.mean(t * n2, -1, keepdims=True))
     gab = lowered(grad_one)
-    s.p5[c, pb, :, :1920] = pack(grad_one)
-    rows5 = PlaneRows(w, s.p5)
     gsm = lowered(nt(gab, chip(SO))).astype(F32)
     gsum = jnp.zeros((3 * PAD, PAD), F32)
     dq, dk, dv = [], [], []
@@ -1165,6 +1161,11 @@
     three = [jnp.concatenate([jnp.concatenate(t, 0), gap], 1) for t in (dq, dk, dv)]
     s.gsg[z] = lowered(join3(three))
     f10 = w.to_z(lambda t: s.gsg.at[z], lambda j: s.gsg.at[z])
+    s.p4[c, pb, :, :1920] = pack(gcq)
+    rows4 = PlaneRows(w, s.p4)
+    s.p5[c, pb, :, :1920] = pack(grad_one)
+    rows5 = PlaneRows(w, s.p5)
+    vred.line()
     s.bias[...] = gsum
 
     def table_head(h, carry):
@@ -1176,7 +1177,6 @@
     s.stz[z] = lax.fori_loop(0, 3, table_head, jnp.zeros((BUCKETS, 128), F32))
     ft = w.to_z(lambda t: s.stz.at[z], lambda j: s.stz.at[z])
     rows2.core()
-    vred.line()
     fo.wait_recv()
     t = r2z + own_d
     for j in range(3):
@@ -1207,10 +1207,10 @@
     ft.wait_recv()
     s.stab[c, pb] = s.stz[0] + s.stz[1] + s.stz[2] + s.stz[3]
     tab_rows = PlaneSmall(w, s.stab)
-    kred.line()
+    vred.spread()
     rows4.relay()
     rows5.relay()
-    vred.spread()
+    kred.line()
     rows2.finish()
     p2 = s.p2
     lhs = inputs_half(unpack(p2, 3072, 256), c)
@@ -1228,9 +1228,9 @@
     fd = w.to_core((s.dgr.at[c], s.dgr.at[c]))
     s.sgain[c, pb] = jnp.concatenate([gain1, gain2, gain3, jnp.zeros((5, WIDTH), F32)], 0)
     gain_rows = PlaneSmall(w, s.sgain)
+    kred.spread()
     rows6.relay()
-    kred.spread()
-    vred.rows.relay()
+    vred.rows.core()
     rows4.core()
     rows5.core()
     t = unpack(p2, 3328, WIDTH).astype(F32)
@@ -1239,8 +1239,6 @@
     out_copies.append(w.local(s.gres, r.gre))
     half_product(s.p4, 768, 4, rows4)
     half_product(s.p5, 768, 3, rows5)
-    vred.rows.core()
-    kred.rows.relay()
     tab_rows.core()
     gain_rows.core()
     fgc.wait_recv()
@@ -1250,8 +1248,8 @@
         for m in (0, 1):
             r.decoder_out[:, 2 * k + m, :] = t[PAD * m : PAD * m + ANS]
             r.decoder_grad[:, 2 * k + m, :] = s.dgr[k, PAD * m : PAD * m + ANS, :]
+    kred.rows.core()
     rows6.core()
-    kred.rows.core()
     vred.rows.finish()
     s.wg[6] = vred.result()
     out_copies.append(w.local(s.wg.at[6], r.squares.at[6]))

time: 132 us -> 126 us (0.955)
  Pallas kernels: 131 us -> 125 us
    pallas_call x1, Pallas kernels: 123 us -> 118 us  [fused(): pl.pallas_call(layer, out_shape=[rows, rows, shape(4, SLOT, WIDTH, kind=B...]
where the time goes in v3:
time: 126 us
  Pallas kernels  125 us (99%)
    pallas_call x1, Pallas kernels, fused(): pl.pallas_call(layer, out_shape=[rows, rows, shape(4, SLOT, WIDTH, kind=B...  118 us
    pallas_call x1, Pallas kernels, fused(): pl.pallas_call(write, out_shape=[*(rows, rows, shape(4, SLOT, WIDTH)), *[...  7.42 us

profile of v3, /device:TPU:1, one launch (start us, length us, event | category | flops | bytes accessed | tf_op | source)
XLA Modules:
  0.0 126.1 jit_solution(9342154388797588831)
XLA Ops:
  0.7 117.9 %shard_map.323 = (f32[20,4,768]{2,1,0:T(4,128)}, f32[20,4,768]{2,1,0:T(4,128)}, bf16[4,512,768]{2,1,0:T(8,128)(2,1)}, bf16[8,96,768]{2,1,0:T(8,128)(2,1)}, bf16[...) custom-call(f32[20,4,768]{2,1,0:T(4,128)} %bitcast.6, ...), custom_call_target="tpu_custom_call" | custom-call | tf_op jit(solution)/shard_map/pallas_call | solution.py:1309
  118.6 7.4 %shard_map.324 = (f32[20,4,768]{2,1,0:T(4,128)}, f32[20,4,768]{2,1,0:T(4,128)}, f32[4,512,768]{2,1,0:T(8,128)}, f32[96,768]{1,0:T(8,128)}, f32[96,768]{1,0:T(8,1...) custom-call(f32[20,4,768]{2,1,0:T(4,128)} %get-tuple-element.42.dout, ...), custom_call_target="tpu_custom_call" | custom-call | tf_op jit(solution)/shard_map/pallas_call | solution.py:1336

commit v4 on v3

--- a/solution.py
+++ b/solution.py
@@ -866,6 +866,7 @@
     f2 = w.to_z(lambda t: s.s2.at[t], lambda j: s.r2.at[j - 1])
     gather_q.core()
     gather_k.plane()
+    gather_v = Gather(w, sq, CV, r.wcv)
 
     f2.wait_recv()
     r1z = xz + own_o
@@ -878,15 +879,14 @@
     tail = jnp.where(lanes(OWN, 256) < 224, high, square - high)
     s.ag2[c, z] = lowered(jnp.where(counts, r1z * g2z, tail))
     f3 = w.to_z(lambda t: s.ag2.at[c, z], lambda j: s.ag2.at[c, z])
-    gather_v = Gather(w, sq, CV, r.wcv)
     gather_k.relay()
+    gather_v.plane()
 
     f3.wait_recv()
     f3c = w.to_core((s.ag2.at[c], s.ag2.at[c]))
     gather_k.core()
     gather_o = Gather(w, sq, CO, r.wco)
     gather_x = Gather(w, sq, EX, r.wex, True)
-    gather_v.plane()
     f3c.wait_recv()
     blocks = [[s.ag2[k, j].astype(F32) for j in range(4)] for k in (0, 1)]
     rs2 = []
@@ -903,8 +903,8 @@
         cq = cq + nn(t, sq[CQ, PART * j : PART * (j + 1), :])
     cq = cq * jnp.concatenate(rs2, 0)
     cq = lowered(cq).astype(F32) * 0.125
+    gather_k.finish()
     gather_v.relay()
-    gather_k.finish()
     held[CK].wait()
     for p in range(6):
         t = jnp.concatenate([pair_stack(cq[PAD * q : PAD * (q + 1)], p) for q in range(4)], 0)
@@ -913,6 +913,7 @@
         for q in range(4):
             s.qk[q, 48 * p : 48 * (p + 1), :] = t[48 * q : 48 * (q + 1)]
     held[EN].wait()
+    gather_v.core()
     s.stat[...] = jnp.zeros((384, 128), F32)
 
     def scores(q, carry):
@@ -934,7 +935,6 @@
     lax.fori_loop(0, 4, scores, 0)
     s.stg[pa] = s.stat[...].T[:8]
     f4 = w.to_column(lambda t: s.stg.at[pa], lambda j: s.stg.at[pa])
-    gather_v.core()
     gather_o.plane()
     gather_x.plane()
     gather_v.finish()
@@ -1207,10 +1207,8 @@
     ft.wait_recv()
     s.stab[c, pb] = s.stz[0] + s.stz[1] + s.stz[2] + s.stz[3]
     tab_rows = PlaneSmall(w, s.stab)
+    kred.line()
     vred.spread()
-    rows4.relay()
-    rows5.relay()
-    kred.line()
     rows2.finish()
     p2 = s.p2
     lhs = inputs_half(unpack(p2, 3072, 256), c)
@@ -1218,6 +1216,8 @@
         cols = slice(WIDTH * j, WIDTH * (j + 1))
         s.gexs[:, cols] = lowered(nn(lhs, unpack(p2, WIDTH * j, WIDTH))[:96])
     out_copies.append(w.local(s.gexs, r.gex))
+    rows4.relay()
+    rows5.relay()
     f11.wait_recv()
     fg.wait_recv()
     fgc = w.to_core((s.dog.at[c], s.dog.at[c]))

time: 126 us -> 124 us (0.984)
  Pallas kernels: 125 us -> 123 us
    pallas_call x1, Pallas kernels: 118 us -> 115 us  [fused(): pl.pallas_call(layer, out_shape=[rows, rows, shape(4, SLOT, WIDTH, kind=B...]
where the time goes in v4:
time: 124 us; the launch traced here: 123 us
  Pallas kernels  123 us (99%)
    pallas_call x1, Pallas kernels, fused(): pl.pallas_call(layer, out_shape=[rows, rows, shape(4, SLOT, WIDTH, kind=B...  115 us
    pallas_call x1, Pallas kernels, fused(): pl.pallas_call(write, out_shape=[*(rows, rows, shape(4, SLOT, WIDTH)), *[...  7.42 us

profile of v4, /device:TPU:1, one launch (start us, length us, event | category | flops | bytes accessed | tf_op | source)
XLA Modules:
  0.0 123.5 jit_solution(10621045760187553426)
XLA Ops:
  0.7 115.2 %shard_map.323 = (f32[20,4,768]{2,1,0:T(4,128)}, f32[20,4,768]{2,1,0:T(4,128)}, bf16[4,512,768]{2,1,0:T(8,128)(2,1)}, bf16[8,96,768]{2,1,0:T(8,128)(2,1)}, bf16[...) custom-call(f32[20,4,768]{2,1,0:T(4,128)} %bitcast.6, ...), custom_call_target="tpu_custom_call" | custom-call | tf_op jit(solution)/shard_map/pallas_call | solution.py:1309
  115.9 7.4 %shard_map.324 = (f32[20,4,768]{2,1,0:T(4,128)}, f32[20,4,768]{2,1,0:T(4,128)}, f32[4,512,768]{2,1,0:T(8,128)}, f32[96,768]{1,0:T(8,128)}, f32[96,768]{1,0:T(8,1...) custom-call(f32[20,4,768]{2,1,0:T(4,128)} %get-tuple-element.42.dout, ...), custom_call_target="tpu_custom_call" | custom-call | tf_op jit(solution)/shard_map/pallas_call | solution.py:1336

commit v5 on v4

--- a/solution.py
+++ b/solution.py
@@ -913,7 +913,6 @@
         for q in range(4):
             s.qk[q, 48 * p : 48 * (p + 1), :] = t[48 * q : 48 * (q + 1)]
     held[EN].wait()
-    gather_v.core()
     s.stat[...] = jnp.zeros((384, 128), F32)
 
     def scores(q, carry):
@@ -932,11 +931,13 @@
         s.stat[:ROWS, :] = jnp.where(lane == q, top, jnp.where(lane == 4 + q, total, old))
         return carry
 
-    lax.fori_loop(0, 4, scores, 0)
+    lax.fori_loop(0, 1, scores, 0)
+    gather_v.core()
+    lax.fori_loop(1, 4, scores, 0)
+    gather_o.plane()
+    gather_x.plane()
     s.stg[pa] = s.stat[...].T[:8]
     f4 = w.to_column(lambda t: s.stg.at[pa], lambda j: s.stg.at[pa])
-    gather_o.plane()
-    gather_x.plane()
     gather_v.finish()
     held[CV].wait()
     other[3].wait_recv()
@@ -1228,8 +1229,8 @@
     fd = w.to_core((s.dgr.at[c], s.dgr.at[c]))
     s.sgain[c, pb] = jnp.concatenate([gain1, gain2, gain3, jnp.zeros((5, WIDTH), F32)], 0)
     gain_rows = PlaneSmall(w, s.sgain)
+    rows6.relay()
     kred.spread()
-    rows6.relay()
     vred.rows.core()
     rows4.core()
     rows5.core()

time: 124 us -> 123 us (level)
  no operation moved by 1% of the time
where the time goes in v5:
time: 123 us
  Pallas kernels  122 us (99%)
    pallas_call x1, Pallas kernels, fused(): pl.pallas_call(layer, out_shape=[rows, rows, shape(4, SLOT, WIDTH, kind=B...  115 us
    pallas_call x1, Pallas kernels, fused(): pl.pallas_call(write, out_shape=[*(rows, rows, shape(4, SLOT, WIDTH)), *[...  7.42 us

profile of v5, /device:TPU:1, one launch (start us, length us, event | category | flops | bytes accessed | tf_op | source)
XLA Modules:
  0.0 122.9 jit_solution(3684176442353621690)
XLA Ops:
  0.7 114.7 %shard_map.323 = (f32[20,4,768]{2,1,0:T(4,128)}, f32[20,4,768]{2,1,0:T(4,128)}, bf16[4,512,768]{2,1,0:T(8,128)(2,1)}, bf16[8,96,768]{2,1,0:T(8,128)(2,1)}, bf16[...) custom-call(f32[20,4,768]{2,1,0:T(4,128)} %bitcast.6, ...), custom_call_target="tpu_custom_call" | custom-call | tf_op jit(solution)/shard_map/pallas_call | solution.py:1310
  115.4 7.4 %shard_map.324 = (f32[20,4,768]{2,1,0:T(4,128)}, f32[20,4,768]{2,1,0:T(4,128)}, f32[4,512,768]{2,1,0:T(8,128)}, f32[96,768]{1,0:T(8,128)}, f32[96,768]{1,0:T(8,1...) custom-call(f32[20,4,768]{2,1,0:T(4,128)} %get-tuple-element.42.dout, ...), custom_call_target="tpu_custom_call" | custom-call | tf_op jit(solution)/shard_map/pallas_call | solution.py:1337
